TPU v7x, 256 devices: a whole 4x4x8 slice. The times are simulated.
256 devices in a mesh: req: 8 (over y, core), chan: 32 (over z, x).
Axes of the slice: x: 4, y: 4, z: 8, core: 2. Of those that a mesh axis runs over, the one named last changes fastest.
Arguments:
- hidden: bfloat16 [1024, 8192], P('req', 'chan'), parts along dimension 0, may hold values from -200 to 200
- norm_gain: bfloat16 [8192], P('chan'), may hold values from 0.099609375 to 1.8984375
- in_weight: bfloat16 [8192, 2, 8192], P(None, None, 'chan'), may hold values from -0.0625 to 0.0625
- conv_weight: float32 [4, 8192], P(None, 'chan'), may hold values from -3 to 3
- conv_bias: float32 [8192], P('chan'), may hold values from -3 to 3
- x_proj_weight: bfloat16 [8192, 544], P('chan'), may hold values from -0.0625 to 0.0625
- dt_norm_gain: float32 [512], replicated, may hold values from 0.1 to 1.9
- b_norm_gain: float32 [16], replicated, may hold values from 0.1 to 1.9
- c_norm_gain: float32 [16], replicated, may hold values from 0.1 to 1.9
- dt_weight: bfloat16 [512, 8192], P(None, 'chan'), may hold values from -0.25 to 0.25
- dt_bias: float32 [8192], P('chan'), may hold values from -2.3 to 0.5
- decay_log: float32 [16, 8192], P(None, 'chan'), may hold values from 0 to 2.77
- skip_gain: float32 [8192], P('chan'), may hold values from 0.5 to 1.5
- conv_state: bfloat16 [1024, 3, 8192], P('req', None, 'chan'), parts along dimension 0, may hold values from -6 to 6
- ssm_state: bfloat16 [1024, 16, 8192], P('req', None, 'chan'), parts along dimension 0, may hold values from -6 to 6
Outputs:
- gated_output: bfloat16 [1024, 8192], P('req', 'chan'), parts along dimension 0
- next_conv_state: bfloat16 [1024, 3, 8192], P('req', None, 'chan'), parts along dimension 0
- next_ssm_state: bfloat16 [1024, 16, 8192], P('req', None, 'chan'), parts along dimension 0
There are 8 independent parts, one for each index of `req`. A program takes and returns all parts, laid end to end along the dimension named above; an argument that names none is the same for every part. Nothing has to cross between parts.
All inputs are finite; a program needn't handle non-finite values.
Results may differ from a plain program's by a relative error of at most 0.0113.
Values may be sent and summed in bfloat16 or wider, within the bound.
A program may use at most 64 MiB of HBM per device.

v0:
```python
import jax
import jax.numpy as jnp
from jax import lax
from jax.sharding import PartitionSpec as P

D = 8192
N = 16
DT_RANK = 512


def rms_scale(values, epsilon):
    return values * lax.rsqrt(jnp.mean(values * values, axis=-1, keepdims=True) + epsilon)


def local(
    hidden,
    norm_gain,
    in_weight,
    conv_weight,
    conv_bias,
    x_proj_weight,
    dt_norm_gain,
    b_norm_gain,
    c_norm_gain,
    dt_weight,
    dt_bias,
    decay_log,
    skip_gain,
    conv_state,
    ssm_state,
):
    local_chan = in_weight.shape[2]
    flat_weight = in_weight.reshape(in_weight.shape[0], 2 * local_chan)
    widened = hidden.astype(jnp.float32)
    row_squares = lax.psum(jnp.sum(widened * widened, axis=1), "chan")
    inverse = lax.rsqrt(row_squares / D + 1e-05)
    normed = (widened * inverse[:, None] * norm_gain.astype(jnp.float32)).astype(jnp.bfloat16)
    projected_in = jnp.dot(
        lax.all_gather(normed, "chan", axis=1, tiled=True),
        flat_weight,
        preferred_element_type=jnp.float32,
    )
    mixed = projected_in.astype(jnp.bfloat16)
    new_inputs = mixed[:, :local_chan]
    gate_half = mixed[:, local_chan:]
    window = jnp.concatenate([conv_state, new_inputs[:, None, :]], axis=1)
    next_conv = window[:, 1:, :]
    conv_out = jnp.sum(window.astype(jnp.float32) * conv_weight[None], axis=1) + conv_bias
    conv_act = jax.nn.silu(conv_out).astype(jnp.bfloat16)
    partial_value = jnp.dot(conv_act, x_proj_weight, preferred_element_type=jnp.float32)
    summed = lax.psum(partial_value, "chan")
    step_normed = (rms_scale(summed[:, :DT_RANK], 1e-06) * dt_norm_gain).astype(jnp.bfloat16)
    b_values = rms_scale(summed[:, DT_RANK : DT_RANK + N], 1e-06) * b_norm_gain
    c_values = rms_scale(summed[:, DT_RANK + N :], 1e-06) * c_norm_gain
    step_size = jax.nn.softplus(
        jnp.dot(step_normed, dt_weight, preferred_element_type=jnp.float32) + dt_bias
    )
    decay_rates = jnp.exp(decay_log)
    decay_factor = jnp.exp(-step_size[:, None, :] * decay_rates[None])
    act_wide = conv_act.astype(jnp.float32)
    new_state = (
        decay_factor * ssm_state.astype(jnp.float32)
        + (step_size * act_wide)[:, None, :] * b_values[:, :, None]
    )
    mixed_out = jnp.sum(new_state * c_values[:, :, None], axis=1) + skip_gain * act_wide
    output = (mixed_out * jax.nn.silu(gate_half.astype(jnp.float32))).astype(jnp.bfloat16)
    return (output, next_conv, new_state.astype(jnp.bfloat16))


def solution(mesh):
    return jax.shard_map(
        local,
        mesh=mesh,
        in_specs=(
            P("req", "chan"),
            P("chan"),
            P(None, None, "chan"),
            P(None, "chan"),
            P("chan"),
            P("chan", None),
            P(),
            P(),
            P(),
            P(None, "chan"),
            P("chan"),
            P(None, "chan"),
            P("chan"),
            P("req", None, "chan"),
            P("req", None, "chan"),
        ),
        out_specs=(P("req", "chan"), P("req", None, "chan"), P("req", None, "chan")),
        check_vma=False,
    )
```

profile of v0, /device:TPU:8, one launch (start us, length us, event | category | flops | bytes accessed | tf_op | source)
XLA Modules:
  0.0 321.4 jit_solution(17333985660358528576)
XLA Ops:
  7.2 0.0 copy-start
  7.2 0.0 all-gather.2.cloned.1.call-start
  7.2 1.0 fusion.2
  8.2 77.7 %psum.14 = f32[128]{0:T(128)S(1)} all-reduce(f32[128]{0:T(128)S(1)} %fusion.2), channel_id=1, replica_groups=mesh['req'=8,'chan'=32] {'chan'}, use_global_device_ids=true, to_apply=%region_1.0 | all-reduce | flops 128 | bytes 1024 | tf_op jit(solution)/shard_map/psum | solution.py:35
  85.9 0.7 convert_element_type.37
  86.6 1.6 fusion.4
  88.1 0.0 all-gather.2.cloned.1.call-update
  88.1 0.0 all-reduce.2.cloned.1.call-start
  88.2 8.0 %copy.20 = bf16[1024,8,2,256]{3,1,2,0:T(8,128)(2,1)} copy(bf16[1024,8,2,256]{3,2,1,0:T(2,128)(2,1)} %bitcast.9) | data formatting | bytes 16777216
  96.2 61.5 %all-gather.2.cloned.1.call-done = bf16[128,8192]{1,0:T(8,128)(2,1)} async-done(((bf16[128,256]{1,0:T(8,128)(2,1)}), bf16[128,8192]{1,0:T(8,128)(2,1)}) %all-gather.2.cloned.1.call-update) | async-done | bytes 2097168 | tf_op jit(solution)/shard_map/all_gather | solution.py:39
  157.7 5.3 %convolution_convert_fusion = bf16[128,512]{1,0:T(8,128)(2,1)S(1)} fusion(bf16[128,8192]{1,0:T(8,128)(2,1)} %all-gather.2.cloned.1.call-done, bf16[8192,512]{1,0:T(8,128)(2,1)} %bitcast.8), kind=kOutput, calls=%fused_computation.3 | convolution fusion | flops 1073807360 | bytes 10616832 | tf_op jit(solution)/shard_map/dot_general | solution.py:38
  163.2 0.1 multiply_reduce_fusion.1
  163.2 1.0 fusion.13
  164.2 0.0 all-reduce.2.cloned.1.call-update
  164.2 0.7 fusion.1
  164.9 142.9 %all-reduce.2.cloned.1.call-done = f32[128,544]{0,1:T(8,128)} async-done(((f32[128,544]{0,1:T(8,128)}), f32[128,544]{0,1:T(8,128)}) %all-reduce.2.cloned.1.call-update) | async-done | bytes 278544 | tf_op jit(solution)/shard_map/psum | solution.py:51
  307.9 0.7 multiply_reduce_fusion.4
  308.6 0.8 multiply_multiply_fusion.1
  309.4 0.1 copy.18
  309.5 0.1 copy.19
  309.6 1.0 multiply_reduce_fusion.2
  310.7 1.3 fusion.14
  312.0 1.8 fusion
  313.8 0.7 fusion.7
  (28 shorter events, 0.1 us)
Async XLA Ops:
  7.2 156.1 %copy-start = (bf16[256,544]{0,1:T(8,128)(2,1)S(1)}, bf16[256,544]{0,1:T(8,128)(2,1)}, u32[]{:S(2)}) copy-start(bf16[256,544]{0,1:T(8,128)(2,1)} %param.20) | copy-start | bytes 835588
  7.2 150.6 %all-gather.2.cloned.1.call-start = ((), (), s32[]{:S(2)}) async-start(), calls=%async_computation | async-start | bytes 2162688 | tf_op jit(solution)/shard_map/all_gather | solution.py:39
  88.1 219.7 %all-reduce.2.cloned.1.call-start = ((), (), s32[]{:S(2)}) async-start(), calls=%async_computation.1 | async-start | bytes 557056 | tf_op jit(solution)/shard_map/psum | solution.py:51
  157.7 5.4 %copy-start.2 = (bf16[128,3,256]{2,0,1:T(8,128)(2,1)S(1)}, bf16[128,3,256]{2,0,1:T(8,128)(2,1)}, u32[]{:S(2)}) copy-start(bf16[128,3,256]{2,0,1:T(8,128)(2,1)} %param.28) | copy-start | bytes 589828
  157.7 5.4 %copy-start.4 = (f32[4,256]{1,0:T(4,128)S(1)}, f32[4,256]{1,0:T(4,128)}, u32[]{:S(2)}) copy-start(f32[4,256]{1,0:T(4,128)} %param.18) | copy-start | bytes 12292
  157.7 5.5 %copy-start.5 = (f32[256]{0:T(256)S(1)}, f32[256]{0:T(256)}, u32[]{:S(2)}) copy-start(f32[256]{0:T(256)} %param.19) | copy-start | bytes 3076
  157.7 6.5 %copy-start.3 = (f32[16,256]{1,0:T(8,128)S(1)}, f32[16,256]{1,0:T(8,128)}, u32[]{:S(2)}) copy-start(f32[16,256]{1,0:T(8,128)} %param.26) | copy-start | bytes 49156
  163.1 145.5 %copy-start.7 = (f32[16]{0:T(128)S(1)}, f32[16]{0:T(128)}, u32[]{:S(2)}) copy-start(f32[16]{0:T(128)} %param.22) | copy-start | bytes 196
  163.1 145.5 %copy-start.8 = (f32[16]{0:T(128)S(1)}, f32[16]{0:T(128)}, u32[]{:S(2)}) copy-start(f32[16]{0:T(128)} %param.23) | copy-start | bytes 196
  163.1 147.6 %copy-start.9 = (bf16[512,256]{1,0:T(8,128)(2,1)S(1)}, bf16[512,256]{1,0:T(8,128)(2,1)}, u32[]{:S(2)}) copy-start(bf16[512,256]{1,0:T(8,128)(2,1)} %param.24) | copy-start | bytes 786436
  163.1 147.6 %copy-start.10 = (f32[512]{0:T(512)S(1)}, f32[512]{0:T(512)}, u32[]{:S(2)}) copy-start(f32[512]{0:T(512)} %param.21) | copy-start | bytes 6148
  163.1 147.6 %copy-start.11 = (f32[256]{0:T(256)S(1)}, f32[256]{0:T(256)}, u32[]{:S(2)}) copy-start(f32[256]{0:T(256)} %param.25) | copy-start | bytes 3076
  163.1 148.9 %copy-start.1 = (bf16[128,16,256]{2,1,0:T(8,128)(2,1)S(1)}, bf16[128,16,256]{2,1,0:T(8,128)(2,1)}, u32[]{:S(2)}) copy-start(bf16[128,16,256]{2,1,0:T(8,128)(2,1)} %param.29) | copy-start | bytes 3145732
  309.6 4.2 %copy-start.6 = (f32[256]{0:T(256)S(1)}, f32[256]{0:T(256)}, u32[]{:S(2)}) copy-start(f32[256]{0:T(256)} %param.27) | copy-start | bytes 3076
Sparse Core Ops, SparseCore 0:
  88.2 69.4 all-gather.1
  164.3 143.4 all-reduce.1
where the time goes:
time: 322 us; the launch traced here: 321 us
  waiting for transfers between devices  204 us (63%)
  blocking collectives  77.7 us (24%)
  between operations  14.2 us (4%)
  other arithmetic  9 us (3%)
  local copies, waits for them, and re-layouts  8.29 us (3%)
  matrix products  7.6 us (2%)
    psum x1, waiting for transfers between devices, local(): summed = lax.psum(partial_value, 'chan')  143 us
    psum x1, blocking collectives, local(): row_squares = lax.psum(jnp.sum(widened * widened, axis=1), 'chan')  77.7 us
    all_gather x1, waiting for transfers between devices, local(): lax.all_gather(normed, 'chan', axis=1, tiled=True)  61.5 us
    unnamed x25, local copies, waits for them, and re-layouts  8.08 us
  transfers between devices with their start and end apart: 2, of which 2 were waited for; matrix products, arithmetic and copies ran while one was open for 3% of the time, Pallas kernels for 0%

commit v1 on v0

v1 whole, which is shorter than its diff:
```python
import jax
import jax.numpy as jnp
from jax import lax
from jax.experimental import pallas as pl
from jax.experimental.pallas import tpu as pltpu
from jax.sharding import PartitionSpec as P

D = 8192
N = 16
DT_RANK = 512
ZS = 8
XS = 4
DEVS = 32
REQ = 128
LOC = 256
MESH = pl.DeviceIdType.MESH
F32 = jnp.float32
BF16 = jnp.bfloat16

OWN = [
    (0, 0, 1), (0, 0, -1), (0, 1, 0), (0, -1, 0), (0, 0, 2),
    (1, 1, 0), (1, -1, 0), (1, 0, 1), (1, 0, -1), (1, 2, 0), (1, -2, 0), (1, 0, 2),
]


def passes():
    along_x = [(0, 1), (0, -1), (0, 2)]
    up, down = [(1, 0)], [(-1, 0)]
    order = [
        ((0, 0, -1), up + down), ((0, 0, 1), up + down), ((0, -1, 0), up), ((0, 1, 0), down),
        ((1, -1, 0), along_x), ((1, 1, 0), along_x), ((1, 0, -1), []), ((1, 0, 1), []),
        ((0, 0, 2), up + down),
        ((1, -2, 0), [(1, 0), (2, 0)] + along_x), ((1, 2, 0), [(-1, 0)] + along_x), ((1, 0, 2), []),
        ((0, -1, -1), up), ((0, 1, -1), down), ((0, -1, 1), up), ((0, 1, 1), down),
        ((1, -1, -1), []), ((1, -1, 1), []),
        ((0, -2, 0), [(1, 0), (2, 0)]), ((0, 2, 0), down),
        ((1, 1, -1), []), ((1, 1, 1), []),
        ((0, -1, 2), up), ((0, 1, 2), down),
        ((1, -3, 0), along_x), ((1, 3, 0), along_x),
        ((1, -1, 2), []), ((1, -2, -1), []), ((1, -2, 1), []),
        ((0, 2, -1), down), ((0, -2, -1), [(1, 0), (2, 0)]), ((1, 2, -1), []), ((0, 2, 1), [(-1, 0), (-2, 0)]),
        ((1, 2, 1), []),
        ((1, 4, 0), along_x), ((0, 3, 0), []), ((1, 1, 2), []), ((0, -2, 1), up), ((1, -2, 2), []),
        ((0, 2, 2), [(-1, 0), (-2, 0)]), ((1, 2, 2), []), ((0, -3, 0), []),
        ((1, -3, -1), []), ((1, -3, 1), []), ((0, 3, -1), []), ((1, 3, -1), []), ((1, 3, 1), []),
        ((0, -2, 2), up), ((0, 3, 1), []), ((0, 4, 0), []), ((1, -3, 2), []), ((1, 4, -1), []), ((1, 4, 1), []),
        ((0, -3, -1), []), ((0, 4, 1), []), ((1, 3, 2), []), ((0, 3, 2), []), ((1, 4, 2), []),
        ((0, -3, 1), []), ((0, 4, -1), []), ((0, 4, 2), []), ((0, -3, 2), []),
    ]
    return order


def gather_kernel(
    hidden, gain, weight_hbm, conv_weight, conv_bias, proj, conv_state,
    act_out, gate_out, conv_out, step_out, bc_out,
    raw, wide, ready, units, total, squares_x, squares_z, part, part_bc, got, got_bc,
    weight_sem, recv_sem, send_sem, sq_sem, sum_sem, out_sem,
):
    req = lax.axis_index("req")
    me = lax.axis_index("chan")
    mz = me // XS
    mx = lax.rem(me, XS)

    def place(dz, dx):
        return lax.rem(mz + dz + ZS, ZS) * XS + lax.rem(mx + dx + XS, XS)

    weight_copies = [
        pltpu.make_async_copy(
            weight_hbm.at[pl.ds(i * 4096, 4096)], raw.at[pl.ds(i * 4096, 4096)], weight_sem.at[i]
        )
        for i in range(8)
    ]
    for copy in weight_copies:
        copy.start()

    greeted = [(1, 0), (-1, 0), (2, 0), (-2, 0), (0, 1), (0, -1), (0, 2)]
    barrier = pltpu.get_barrier_semaphore()
    for dz, dx in greeted:
        pl.semaphore_signal(barrier, inc=1, device_id=(req, place(dz, dx)), device_id_type=MESH)

    widened = hidden[...].astype(F32)
    scaled = (widened * gain[...].astype(F32)).astype(BF16)
    units[0, pl.ds(me, 1)] = scaled[None, :, :128]
    units[1, pl.ds(me, 1)] = scaled[None, :, 128:]
    square_row = lax.dot_general(
        jnp.ones((8, LOC), F32), widened * widened, (((1,), (1,)), ((), ())),
        precision=lax.Precision.HIGHEST, preferred_element_type=F32,
    )
    squares_x[pl.ds(mx, 1)] = square_row[None, :1]

    pl.semaphore_wait(barrier, len(greeted))

    def push(half, dz, dx, hz, hx):
        owner = place(dz, dx)
        pltpu.make_async_remote_copy(
            units.at[half, owner], units.at[half, owner], send_sem.at[half],
            recv_sem.at[half, (dz - hz) % ZS, (dx - hx) % XS],
            device_id=(req, place(hz, hx)), device_id_type=MESH,
        ).start()

    def await_unit(half, dz, dx):
        owner = place(dz, dx)
        pltpu.make_async_copy(
            units.at[half, owner], units.at[half, owner], recv_sem.at[half, dz % ZS, dx % XS]
        ).wait()

    for half, hz, hx in OWN:
        push(half, 0, 0, hz, hx)
    for dx in (1, -1, 2):
        pltpu.make_async_remote_copy(
            squares_x.at[mx], squares_x.at[mx], sq_sem.at[0], sq_sem.at[1],
            device_id=(req, place(0, dx)), device_id_type=MESH,
        ).start()

    def convert(index, _):
        wide[...] = raw[pl.ds(pl.multiple_of(index * 1024, 1024), 1024), :].astype(F32)
        for side in range(2):
            for tile in range(2):
                column = side * 256 + tile * 128
                ready[pl.ds(pl.multiple_of(index * 256, 256), 256), column : column + 128] = wide[
                    pl.ds(2 * tile + side, 256, stride=4), :
                ].astype(BF16)
        return 0

    def multiply(dz, dx, first=False):
        owner = place(dz, dx)
        left = jnp.concatenate([units[0, owner], units[1, owner]], axis=1)
        product = jnp.dot(
            left, ready[pl.ds(pl.multiple_of(owner * 256, 256), 256), :], preferred_element_type=F32
        )
        total[...] = product if first else total[...] + product

    converted = 0

    def convert_to(count):
        nonlocal converted
        while converted < count:
            if converted % 4 == 0:
                weight_copies[converted // 4].wait()
            last = min(count, converted // 4 * 4 + 4)
            lax.fori_loop(converted, last, convert, 0)
            converted = last

    convert_to(8)
    arrived = {}
    pending = []
    started = False
    column = 0
    order = passes()
    for step, ((half, dz, dx), hops) in enumerate(order):
        await_unit(half, dz, dx)
        for hz, hx in hops:
            push(half, dz, dx, hz, hx)
        arrived[(dz, dx)] = arrived.get((dz, dx), 0) + 1
        if arrived[(dz, dx)] == 2:
            pending.append((dz, dx))
        if dx == 0 and half == 1:
            column += 1
            if column == 7:
                pltpu.make_async_copy(
                    squares_x.at[pl.ds(0, 3)], squares_x.at[pl.ds(0, 3)], sq_sem.at[1]
                ).wait()
                squares_z[pl.ds(mz, 1)] = jnp.sum(squares_x[...], axis=0, keepdims=True)
                for hz in (1, -1, 2, -2, 3, -3, 4):
                    pltpu.make_async_remote_copy(
                        squares_z.at[mz], squares_z.at[mz], sq_sem.at[2], sq_sem.at[3],
                        device_id=(req, place(hz, 0)), device_id_type=MESH,
                    ).start()
        if converted < DEVS:
            convert_to(min(DEVS, converted + 2))
        elif pending:
            if not started:
                multiply(0, 0, True)
                started = True
            multiply(*pending.pop(0))
    while pending:
        multiply(*pending.pop(0))

    pltpu.make_async_copy(squares_z.at[pl.ds(0, 7)], squares_z.at[pl.ds(0, 7)], sq_sem.at[3]).wait()
    row = jnp.sum(squares_z[...], axis=0)
    inverse_row = lax.rsqrt(row / D + 1e-05)
    inverse = jnp.transpose(jnp.broadcast_to(inverse_row, (128, 128)))
    mixed = [
        (total[:, i * 128 : i * 128 + 128] * inverse).astype(BF16) for i in range(4)
    ]
    new_inputs = jnp.concatenate(mixed[:2], axis=1)
    gate_out[...] = jnp.concatenate(mixed[2:], axis=1)
    conv_out[0] = conv_state[1]
    conv_out[1] = conv_state[2]
    conv_out[2] = new_inputs
    window = conv_state[0].astype(F32) * conv_weight[0:1]
    window += conv_state[1].astype(F32) * conv_weight[1:2]
    window += conv_state[2].astype(F32) * conv_weight[2:3]
    window += new_inputs.astype(F32) * conv_weight[3:4]
    window += conv_bias[...]
    act = (window * jax.nn.sigmoid(window)).astype(BF16)
    act_out[...] = act
    projected = lax.dot_general(
        proj[...], act, (((1,), (1,)), ((), ())), preferred_element_type=F32
    )
    part[...] = projected[:DT_RANK].astype(BF16)
    for i in range(2 * N):
        part_bc[i] = projected[DT_RANK + i : DT_RANK + i + 1]

    def rows(index):
        return pl.ds(pl.multiple_of(index * 16, 16), 16)

    def spread(i, _):
        peer = lax.rem(me + i, DEVS)
        pltpu.make_async_remote_copy(
            part.at[rows(peer)], got.at[rows(me)], sum_sem.at[0], sum_sem.at[1],
            device_id=(req, peer), device_id_type=MESH,
        ).start()
        pltpu.make_async_remote_copy(
            part_bc.at[peer], got_bc.at[me], sum_sem.at[2], sum_sem.at[3],
            device_id=(req, peer), device_id_type=MESH,
        ).start()
        return 0

    lax.fori_loop(1, DEVS, spread, 0)
    got[rows(me), :] = part[rows(me), :]
    got_bc[pl.ds(me, 1)] = part_bc[pl.ds(me, 1)]

    some, some_bc = pl.ds(0, 31 * 16), pl.ds(0, 31)
    pltpu.make_async_copy(got.at[some], got.at[some], sum_sem.at[1]).wait()
    pltpu.make_async_copy(got_bc.at[some_bc], got_bc.at[some_bc], sum_sem.at[3]).wait()
    step = got[0:16].astype(F32)
    for i in range(1, DEVS):
        step += got[i * 16 : i * 16 + 16].astype(F32)
    step_out[rows(me), :] = step.astype(BF16)
    bc_out[pl.ds(me, 1)] = jnp.sum(got_bc[...], axis=0, keepdims=True)

    def share(i, _):
        peer = lax.rem(me + i, DEVS)
        pltpu.make_async_remote_copy(
            step_out.at[rows(me)], step_out.at[rows(me)], out_sem.at[0], out_sem.at[1],
            device_id=(req, peer), device_id_type=MESH,
        ).start()
        pltpu.make_async_remote_copy(
            bc_out.at[me], bc_out.at[me], out_sem.at[2], out_sem.at[3],
            device_id=(req, peer), device_id_type=MESH,
        ).start()
        return 0

    lax.fori_loop(1, DEVS, share, 0)
    for half in range(2):
        pltpu.make_async_copy(
            units.at[half, pl.ds(0, 31)], units.at[half, pl.ds(0, 31)], send_sem.at[half]
        ).wait()
    pltpu.make_async_copy(squares_x.at[pl.ds(0, 3)], squares_x.at[pl.ds(0, 3)], sq_sem.at[0]).wait()
    pltpu.make_async_copy(squares_z.at[pl.ds(0, 7)], squares_z.at[pl.ds(0, 7)], sq_sem.at[2]).wait()
    for i in (0, 2):
        pltpu.make_async_copy(
            (got if i == 0 else got_bc).at[some if i == 0 else some_bc],
            (got if i == 0 else got_bc).at[some if i == 0 else some_bc],
            sum_sem.at[i],
        ).wait()
    for i in range(4):
        ref, span = (step_out, some) if i < 2 else (bc_out, some_bc)
        pltpu.make_async_copy(ref.at[span], ref.at[span], out_sem.at[i]).wait()


def front(hidden, norm_gain, in_weight, conv_weight, conv_bias, x_proj_weight, conv_state):
    weight = in_weight.reshape(D, 2, 2, 128).transpose(0, 2, 1, 3).reshape(4 * D, 128)
    vmem = pl.BlockSpec(memory_space=pltpu.VMEM)
    return pl.pallas_call(
        gather_kernel,
        out_shape=(
            jax.ShapeDtypeStruct((REQ, LOC), BF16),
            jax.ShapeDtypeStruct((REQ, LOC), BF16),
            jax.ShapeDtypeStruct((3, REQ, LOC), BF16),
            jax.ShapeDtypeStruct((DT_RANK, REQ), BF16),
            jax.ShapeDtypeStruct((2 * N, 1, REQ), F32),
        ),
        in_specs=[vmem, vmem, pl.BlockSpec(memory_space=pl.ANY), vmem, vmem, vmem, vmem],
        out_specs=(vmem,) * 5,
        scratch_shapes=[
            pltpu.VMEM((4 * D, 128), BF16),
            pltpu.VMEM((1024, 128), F32),
            pltpu.VMEM((D, 2 * LOC), BF16),
            pltpu.VMEM((2, DEVS, REQ, 128), BF16),
            pltpu.VMEM((REQ, 2 * LOC), F32),
            pltpu.VMEM((XS, 1, REQ), F32),
            pltpu.VMEM((ZS, 1, REQ), F32),
            pltpu.VMEM((DT_RANK, REQ), BF16),
            pltpu.VMEM((2 * N, 1, REQ), F32),
            pltpu.VMEM((DT_RANK, REQ), BF16),
            pltpu.VMEM((DEVS, 1, REQ), F32),
            pltpu.SemaphoreType.DMA((8,)),
            pltpu.SemaphoreType.DMA((2, ZS, XS)),
            pltpu.SemaphoreType.DMA((2,)),
            pltpu.SemaphoreType.DMA((4,)),
            pltpu.SemaphoreType.DMA((4,)),
            pltpu.SemaphoreType.DMA((4,)),
        ],
        compiler_params=pltpu.CompilerParams(
            collective_id=0, has_side_effects=True, vmem_limit_bytes=50 * 2**20
        ),
    )(
        hidden,
        norm_gain.reshape(1, LOC),
        weight,
        conv_weight,
        conv_bias.reshape(1, LOC),
        x_proj_weight.T,
        conv_state.transpose(1, 0, 2),
    )


def rms_scale(values, epsilon, axis):
    return values * lax.rsqrt(jnp.mean(values * values, axis=axis, keepdims=True) + epsilon)


def local(
    hidden,
    norm_gain,
    in_weight,
    conv_weight,
    conv_bias,
    x_proj_weight,
    dt_norm_gain,
    b_norm_gain,
    c_norm_gain,
    dt_weight,
    dt_bias,
    decay_log,
    skip_gain,
    conv_state,
    ssm_state,
):
    conv_act, gate_half, next_conv, step_raw, bc_raw = front(
        hidden, norm_gain, in_weight, conv_weight, conv_bias, x_proj_weight, conv_state
    )
    bc_raw = bc_raw.reshape(2 * N, REQ)
    step_normed = (
        rms_scale(step_raw.astype(F32), 1e-06, 0) * dt_norm_gain[:, None]
    ).astype(BF16)
    b_values = (rms_scale(bc_raw[:N], 1e-06, 0) * b_norm_gain[:, None]).T
    c_values = (rms_scale(bc_raw[N:], 1e-06, 0) * c_norm_gain[:, None]).T
    step_size = jax.nn.softplus(
        jnp.dot(step_normed.T, dt_weight, preferred_element_type=F32) + dt_bias
    )
    decay_rates = jnp.exp(decay_log)
    decay_factor = jnp.exp(-step_size[:, None, :] * decay_rates[None])
    act_wide = conv_act.astype(F32)
    new_state = (
        decay_factor * ssm_state.astype(F32)
        + (step_size * act_wide)[:, None, :] * b_values[:, :, None]
    )
    mixed_out = jnp.sum(new_state * c_values[:, :, None], axis=1) + skip_gain * act_wide
    output = (mixed_out * jax.nn.silu(gate_half.astype(F32))).astype(BF16)
    return (output, next_conv.transpose(1, 0, 2), new_state.astype(BF16))


def solution(mesh):
    return jax.shard_map(
        local,
        mesh=mesh,
        in_specs=(
            P("req", "chan"),
            P("chan"),
            P(None, None, "chan"),
            P(None, "chan"),
            P("chan"),
            P("chan", None),
            P(),
            P(),
            P(),
            P(None, "chan"),
            P("chan"),
            P(None, "chan"),
            P("chan"),
            P("req", None, "chan"),
            P("req", None, "chan"),
        ),
        out_specs=(P("req", "chan"), P("req", None, "chan"), P("req", None, "chan")),
        check_vma=False,
    )
```

time: 322 us -> 54.6 us (0.17)
  waiting for transfers between devices: 204 us -> 0 us
  blocking collectives: 77.7 us -> 0 us
  Pallas kernels: 0 us -> 44 us
  between operations: 14.2 us -> 0.74 us
  matrix products: 7.6 us -> 0.39 us
  other arithmetic: 9 us -> 2.73 us
    psum x1 -> x0, waiting for transfers between devices: 143 us -> none  [local(): summed = lax.psum(partial_value, 'chan')]
    psum x1 -> x0, blocking collectives: 77.7 us -> none  [local(): row_squares = lax.psum(jnp.sum(widened * widened, axis=1), 'chan')]
    all_gather x1 -> x0, waiting for transfers between devices: 61.5 us -> none  [local(): lax.all_gather(normed, 'chan', axis=1, tiled=True)]
    pallas_call x0 -> x1, Pallas kernels: none -> 44 us  [front(): pl.pallas_call(gather_kernel, out_shape=(jax.ShapeDtypeStruct((REQ, LOC),...]
    dot_general x3 -> x1, matrix products: 7.6 us -> 0.39 us  [local(): jnp.dot(step_normed.T, dt_weight, preferred_element_type=F32) + dt_bias]
    unnamed x25, local copies, waits for them, and re-layouts: 8.08 us -> 4.8 us
  transfers between devices with their start and end apart: 2 -> 0, of which waited for: 2 -> 0; matrix products, arithmetic and copies ran while one was open for 3% -> 0% of each run, Pallas kernels for 0% -> 0%
where the time goes in v1:
time: 54.6 us; the launch traced here: 54.3 us
  Pallas kernels  44 us (81%)
  local copies, waits for them, and re-layouts  6.43 us (12%)
  other arithmetic  2.73 us (5%)
  between operations  0.74 us (1%)
    pallas_call x1, Pallas kernels, front(): pl.pallas_call(gather_kernel, out_shape=(jax.ShapeDtypeStruct((REQ, LOC),...  44 us
    unnamed x25, local copies, waits for them, and re-layouts  4.8 us
    convert_element_type x1, other arithmetic, local(): return (output, next_conv.transpose(1, 0, 2), new_state.astype(BF16))  1.76 us

profile of v1, /device:TPU:8, one launch (start us, length us, event | category | flops | bytes accessed | tf_op | source)
XLA Modules:
  0.0 54.3 jit_solution(15687847566881724912)
XLA Ops:
  0.6 0.0 copy-start
  0.6 0.7 %reshape.56.gain = bf16[1,256]{1,0:T(2,128)(2,1)S(1)} reshape(bf16[256]{0:T(256)(128)(2,1)} %param.16) | data formatting | bytes 1024 | tf_op jit(solution)/shard_map/reshape | solution.py:301
  1.3 0.7 %exp.15 = f32[16,256]{1,0:T(8,128)S(1)} exponential(f32[16,256]{1,0:T(8,128)} %param.26) | non-fusion elementwise | bytes 32768 | tf_op jit(solution)/shard_map/exp | solution.py:343
  2.1 1.0 %copy-done.1 = bf16[256,544]{0,1:T(8,128)(2,1)S(1)} copy-done((bf16[256,544]{0,1:T(8,128)(2,1)S(1)}, bf16[256,544]{0,1:T(8,128)(2,1)}, u32[]{:S(2)}) %copy-start.1) | copy-done | bytes 278552
  3.0 0.9 %copy-done.2 = bf16[128,3,256]{2,0,1:T(8,128)(2,1)S(1)} copy-done((bf16[128,3,256]{2,0,1:T(8,128)(2,1)S(1)}, bf16[128,3,256]{2,0,1:T(8,128)(2,1)}, u32[]{:S(2)}) %copy-start.2) | copy-done | bytes 196632
  4.0 0.8 %copy-done.3 = bf16[128,256]{1,0:T(8,128)(2,1)S(1)} copy-done((bf16[128,256]{1,0:T(8,128)(2,1)S(1)}, bf16[128,256]{1,0:T(8,128)(2,1)}, u32[]{:S(2)}) %copy-start.3) | copy-done | bytes 65560
  4.8 0.7 %copy-done.4 = f32[4,256]{1,0:T(4,128)S(1)} copy-done((f32[4,256]{1,0:T(4,128)S(1)}, f32[4,256]{1,0:T(4,128)}, u32[]{:S(2)}) %copy-start.4) | copy-done | bytes 4120
  5.5 0.7 %copy-done.5 = f32[256]{0:T(256)S(1)} copy-done((f32[256]{0:T(256)S(1)}, f32[256]{0:T(256)}, u32[]{:S(2)}) %copy-start.5) | copy-done | bytes 1048
  6.2 0.0 copy-start.6
  6.2 44.0 %shard_map.166 = (bf16[128,256]{1,0:T(8,128)(2,1)S(1)}, bf16[128,256]{1,0:T(8,128)(2,1)S(1)}, bf16[3,128,256]{2,1,0:T(8,128)(2,1)S(1)}, bf16[512,128]{1,0:T(8,128)(2,1)S(1)}, f32[32,1,128]{2,1,0:T(1,128)S(1)}) custom-call(bf16[128,256]{1,0:T(8,128)(2,1)S(1)} %copy-done.3, bf16[1,256]{1,0:T(2,128)(2,1)S(1)} %reshape.56.gain, bf16[32768,128]{1,0:T(8,128)(2,1)} %bitcast.20, ...), custom_call_target="tpu_custom_call" | custom-call | tf_op jit(solution)/shard_map/pallas_call | solution.py:266
  50.2 0.0 copy-start.7
  50.3 0.0 copy-done.8
  50.3 0.1 multiply_bitcast_fusion
  50.4 0.0 copy-done.9
  50.4 0.1 multiply_bitcast_fusion.1
  50.5 0.1 fusion.1
  50.6 0.1 copy.19
  50.7 0.1 copy.20
  50.8 0.0 copy-done
  50.8 0.0 copy-done.10
  50.8 0.4 fusion.15
  51.2 1.8 %fusion = (bf16[128,16,256]{2,1,0:T(8,128)(2,1)}, f32[128,256]{1,0:T(8,128)S(1)}) fusion(bf16[128,16,256]{2,1,0:T(8,128)(2,1)S(1)} %copy-done.6, f32[128,16]{1,0:T(8,128)S(1)} %copy.19, f32[128,256]{1,0:T(8,128)S(1)} %get-tuple-element.16, f32[16,256]{1,0:T(8,128)S(1)} %exp.15, f32[128,256]{1,0:T(8,128)S(1)} %get-tuple-element.15, f32[128,16]{1,0:T(8,128)S(1)} %copy.20), kind=kLoop, calls=%fused_computation.2 | loop fusion | flops 4161536 | bytes 2523136 | tf_op jit(solution)/shard_map/convert_element_type | solution.py:352
  53.0 0.7 %fusion.6 = bf16[128,256]{1,0:T(8,128)(2,1)} fusion(f32[128,256]{1,0:T(8,128)S(1)} %get-tuple-element.14, bf16[128,256]{1,0:T(8,128)(2,1)S(1)} %get-tuple-element.9, bf16[128,256]{1,0:T(8,128)(2,1)S(1)} %get-tuple-element.11, f32[256]{0:T(256)S(1)} %copy-done.7), kind=kLoop, calls=%fused_computation.16 | loop fusion | flops 327680 | bytes 328704 | tf_op jit(solution)/shard_map/convert_element_type | solution.py:351
  53.6 0.7 %copy.22 = bf16[128,3,256]{2,0,1:T(8,128)(2,1)} copy(bf16[128,3,256]{2,0,1:T(8,128)(2,1)S(1)} %bitcast.17) | data formatting | bytes 393216
  (18 shorter events, 0.1 us)
Async XLA Ops:
  0.6 50.1 %copy-start = (bf16[512,256]{1,0:T(8,128)(2,1)S(1)}, bf16[512,256]{1,0:T(8,128)(2,1)}, u32[]{:S(2)}) copy-start(bf16[512,256]{1,0:T(8,128)(2,1)} %param.24) | copy-start | bytes 786436
  2.1 1.0 %copy-start.1 = (bf16[256,544]{0,1:T(8,128)(2,1)S(1)}, bf16[256,544]{0,1:T(8,128)(2,1)}, u32[]{:S(2)}) copy-start(bf16[256,544]{0,1:T(8,128)(2,1)} %param.20) | copy-start | bytes 835588
  3.0 0.9 %copy-start.2 = (bf16[128,3,256]{2,0,1:T(8,128)(2,1)S(1)}, bf16[128,3,256]{2,0,1:T(8,128)(2,1)}, u32[]{:S(2)}) copy-start(bf16[128,3,256]{2,0,1:T(8,128)(2,1)} %param.28) | copy-start | bytes 589828
  4.0 0.8 %copy-start.3 = (bf16[128,256]{1,0:T(8,128)(2,1)S(1)}, bf16[128,256]{1,0:T(8,128)(2,1)}, u32[]{:S(2)}) copy-start(bf16[128,256]{1,0:T(8,128)(2,1)} %hidden.1) | copy-start | bytes 196612
  4.8 0.7 %copy-start.4 = (f32[4,256]{1,0:T(4,128)S(1)}, f32[4,256]{1,0:T(4,128)}, u32[]{:S(2)}) copy-start(f32[4,256]{1,0:T(4,128)} %conv_weight.1) | copy-start | bytes 12292
  5.5 0.7 %copy-start.5 = (f32[256]{0:T(256)S(1)}, f32[256]{0:T(256)}, u32[]{:S(2)}) copy-start(f32[256]{0:T(256)} %param.19) | copy-start | bytes 3076
  6.2 44.1 %copy-start.8 = (f32[16]{0:T(128)S(1)}, f32[16]{0:T(128)}, u32[]{:S(2)}) copy-start(f32[16]{0:T(128)} %param.23) | copy-start | bytes 196
  6.2 44.2 %copy-start.9 = (f32[16]{0:T(128)S(1)}, f32[16]{0:T(128)}, u32[]{:S(2)}) copy-start(f32[16]{0:T(128)} %param.22) | copy-start | bytes 196
  6.2 44.6 %copy-start.10 = (f32[512]{0:T(512)S(1)}, f32[512]{0:T(512)}, u32[]{:S(2)}) copy-start(f32[512]{0:T(512)} %param.21) | copy-start | bytes 6148
  6.2 44.6 %copy-start.11 = (f32[256]{0:T(256)S(1)}, f32[256]{0:T(256)}, u32[]{:S(2)}) copy-start(f32[256]{0:T(256)} %param.25) | copy-start | bytes 3076
  6.2 45.0 %copy-start.6 = (bf16[128,16,256]{2,1,0:T(8,128)(2,1)S(1)}, bf16[128,16,256]{2,1,0:T(8,128)(2,1)}, u32[]{:S(2)}) copy-start(bf16[128,16,256]{2,1,0:T(8,128)(2,1)} %param.29) | copy-start | bytes 3145732
  50.2 2.7 %copy-start.7 = (f32[256]{0:T(256)S(1)}, f32[256]{0:T(256)}, u32[]{:S(2)}) copy-start(f32[256]{0:T(256)} %param.27) | copy-start | bytes 3076

commit v2 on v1

--- a/solution.py
+++ b/solution.py
@@ -51,10 +51,10 @@
 
 
 def gather_kernel(
-    hidden, gain, weight_hbm, conv_weight, conv_bias, proj, conv_state,
-    act_out, gate_out, conv_out, step_out, bc_out,
-    raw, wide, ready, units, total, squares_x, squares_z, part, part_bc, got, got_bc,
-    weight_sem, recv_sem, send_sem, sq_sem, sum_sem, out_sem,
+    hidden_hbm, gain_hbm, weight_hbm, conv_weight_hbm, conv_bias_hbm, proj_hbm, conv_state_hbm,
+    act_out, mixed_out, step_out, bc_out,
+    hidden, gain, conv_weight, conv_bias, proj, conv_state, raw, wide, ready, units, total, squares_x, squares_z, part, part_bc, got, got_bc,
+    in_sem, weight_sem, recv_sem, send_sem, sq_sem, sum_sem, out_sem,
 ):
     req = lax.axis_index("req")
     me = lax.axis_index("chan")
@@ -64,24 +64,43 @@
     def place(dz, dx):
         return lax.rem(mz + dz + ZS, ZS) * XS + lax.rem(mx + dx + XS, XS)
 
+    small_copies = [
+        pltpu.make_async_copy(source, target, in_sem.at[i])
+        for i, (source, target) in enumerate(
+            (
+                (hidden_hbm, hidden),
+                (gain_hbm, gain),
+                (conv_weight_hbm, conv_weight),
+                (conv_bias_hbm, conv_bias),
+                (proj_hbm, proj),
+                (conv_state_hbm, conv_state),
+            )
+        )
+    ]
+    small_copies[0].start()
+    small_copies[1].start()
     weight_copies = [
         pltpu.make_async_copy(
             weight_hbm.at[pl.ds(i * 4096, 4096)], raw.at[pl.ds(i * 4096, 4096)], weight_sem.at[i]
         )
         for i in range(8)
     ]
-    for copy in weight_copies:
-        copy.start()
-
     greeted = [(1, 0), (-1, 0), (2, 0), (-2, 0), (0, 1), (0, -1), (0, 2)]
     barrier = pltpu.get_barrier_semaphore()
     for dz, dx in greeted:
         pl.semaphore_signal(barrier, inc=1, device_id=(req, place(dz, dx)), device_id_type=MESH)
 
+    for copy in weight_copies:
+        copy.start()
+    for copy in small_copies[2:]:
+        copy.start()
+    small_copies[0].wait()
+    small_copies[1].wait()
     widened = hidden[...].astype(F32)
-    scaled = (widened * gain[...].astype(F32)).astype(BF16)
-    units[0, pl.ds(me, 1)] = scaled[None, :, :128]
-    units[1, pl.ds(me, 1)] = scaled[None, :, 128:]
+    gain_rows = gain[...].astype(F32)
+    for half in range(2):
+        scaled = widened[:, half * 128 : half * 128 + 128] * gain_rows[half : half + 1]
+        units[half, pl.ds(me, 1)] = scaled.astype(BF16)[None]
     square_row = lax.dot_general(
         jnp.ones((8, LOC), F32), widened * widened, (((1,), (1,)), ((), ())),
         precision=lax.Precision.HIGHEST, preferred_element_type=F32,
@@ -180,14 +199,13 @@
     row = jnp.sum(squares_z[...], axis=0)
     inverse_row = lax.rsqrt(row / D + 1e-05)
     inverse = jnp.transpose(jnp.broadcast_to(inverse_row, (128, 128)))
+    for copy in small_copies[2:]:
+        copy.wait()
     mixed = [
         (total[:, i * 128 : i * 128 + 128] * inverse).astype(BF16) for i in range(4)
     ]
     new_inputs = jnp.concatenate(mixed[:2], axis=1)
-    gate_out[...] = jnp.concatenate(mixed[2:], axis=1)
-    conv_out[0] = conv_state[1]
-    conv_out[1] = conv_state[2]
-    conv_out[2] = new_inputs
+    mixed_out[...] = jnp.concatenate(mixed, axis=1)
     window = conv_state[0].astype(F32) * conv_weight[0:1]
     window += conv_state[1].astype(F32) * conv_weight[1:2]
     window += conv_state[2].astype(F32) * conv_weight[2:3]
@@ -266,15 +284,20 @@
     return pl.pallas_call(
         gather_kernel,
         out_shape=(
-            jax.ShapeDtypeStruct((REQ, LOC), BF16),
-            jax.ShapeDtypeStruct((REQ, LOC), BF16),
-            jax.ShapeDtypeStruct((3, REQ, LOC), BF16),
-            jax.ShapeDtypeStruct((DT_RANK, REQ), BF16),
-            jax.ShapeDtypeStruct((2 * N, 1, REQ), F32),
+            pltpu.VMEM((REQ, LOC), BF16),
+            pltpu.VMEM((REQ, 2 * LOC), BF16),
+            pltpu.VMEM((DT_RANK, REQ), BF16),
+            pltpu.VMEM((2 * N, 1, REQ), F32),
         ),
-        in_specs=[vmem, vmem, pl.BlockSpec(memory_space=pl.ANY), vmem, vmem, vmem, vmem],
-        out_specs=(vmem,) * 5,
+        in_specs=[pl.BlockSpec(memory_space=pltpu.HBM)] * 7,
+        out_specs=(vmem,) * 4,
         scratch_shapes=[
+            pltpu.VMEM((REQ, LOC), BF16),
+            pltpu.VMEM((2, 128), BF16),
+            pltpu.VMEM((4, LOC), F32),
+            pltpu.VMEM((1, LOC), F32),
+            pltpu.VMEM((DT_RANK + 2 * N, LOC), BF16),
+            pltpu.VMEM((3, REQ, LOC), BF16),
             pltpu.VMEM((4 * D, 128), BF16),
             pltpu.VMEM((1024, 128), F32),
             pltpu.VMEM((D, 2 * LOC), BF16),
@@ -286,6 +309,7 @@
             pltpu.VMEM((2 * N, 1, REQ), F32),
             pltpu.VMEM((DT_RANK, REQ), BF16),
             pltpu.VMEM((DEVS, 1, REQ), F32),
+            pltpu.SemaphoreType.DMA((6,)),
             pltpu.SemaphoreType.DMA((8,)),
             pltpu.SemaphoreType.DMA((2, ZS, XS)),
             pltpu.SemaphoreType.DMA((2,)),
@@ -294,11 +318,11 @@
             pltpu.SemaphoreType.DMA((4,)),
         ],
         compiler_params=pltpu.CompilerParams(
-            collective_id=0, has_side_effects=True, vmem_limit_bytes=50 * 2**20
+            collective_id=0, has_side_effects=True, vmem_limit_bytes=56 * 2**20
         ),
     )(
         hidden,
-        norm_gain.reshape(1, LOC),
+        norm_gain.reshape(2, 128),
         weight,
         conv_weight,
         conv_bias.reshape(1, LOC),
@@ -307,8 +331,55 @@
     )
 
 
-def rms_scale(values, epsilon, axis):
-    return values * lax.rsqrt(jnp.mean(values * values, axis=axis, keepdims=True) + epsilon)
+BLOCKS = 4
+ROWS = REQ // BLOCKS
+
+
+def state_kernel(
+    act, mixed, step_raw, bc_raw, dt_gain, b_gain, c_gain, dt_weight, dt_bias, decay_log, skip_gain, conv_state, state,
+    out, next_conv, next_state,
+    step_size, drive, b_turned, c_turned,
+):
+    block = pl.program_id(0)
+
+    @pl.when(block == 0)
+    def _():
+        raw = step_raw[...].astype(F32)
+        scale = lax.rsqrt(jnp.mean(raw * raw, axis=0, keepdims=True) + 1e-06)
+        normed = (jnp.transpose(raw * scale) * dt_gain[...]).astype(BF16)
+        before = jnp.dot(normed, dt_weight[...], preferred_element_type=F32) + dt_bias[...]
+        size = jnp.maximum(before, 0.0) + jnp.log1p(jnp.exp(-jnp.abs(before)))
+        step_size[...] = size
+        drive[...] = size * act[...].astype(F32)
+        square = (N, N)
+        eye = lax.broadcasted_iota(jnp.int32, square, 0) == lax.broadcasted_iota(jnp.int32, square, 1)
+        for part, gain_row, turned in ((0, b_gain, b_turned), (N, c_gain, c_turned)):
+            column = jnp.sum(
+                jnp.where(eye, jnp.broadcast_to(gain_row[...], square), 0.0), axis=1, keepdims=True
+            )
+            values = bc_raw[part : part + N]
+            scale = lax.rsqrt(jnp.mean(values * values, axis=0, keepdims=True) + 1e-06)
+            values = values * scale * column
+            for i in range(BLOCKS):
+                turned[i] = pltpu.roll(values, REQ - i * ROWS, 1) if i else values
+
+    rows = pl.ds(pl.multiple_of(block * ROWS, ROWS), ROWS)
+    rates = -jnp.exp(decay_log[...])
+    b_here = b_turned[block]
+    c_here = c_turned[block]
+    sums = []
+    for r in range(ROWS):
+        row = pl.ds(block * ROWS + r, 1)
+        decay = jnp.exp(step_size[row, :] * rates)
+        new = decay * state[r].astype(F32) + drive[row, :] * b_here[:, r : r + 1]
+        next_state[r] = new.astype(BF16)
+        sums.append(jnp.sum(new * c_here[:, r : r + 1], axis=0, keepdims=True))
+    summed = jnp.concatenate(sums, axis=0)
+    act_wide = act[rows, :].astype(F32)
+    gate = mixed[rows, LOC:].astype(F32)
+    out[...] = ((summed + skip_gain[...] * act_wide) * (gate * jax.nn.sigmoid(gate))).astype(BF16)
+    next_conv[0:2] = conv_state[1:3, rows, :]
+    next_conv[2] = mixed[rows, :LOC]
 
 
 def local(
@@ -328,28 +399,47 @@
     conv_state,
     ssm_state,
 ):
-    conv_act, gate_half, next_conv, step_raw, bc_raw = front(
+    act, mixed, step_raw, bc_raw = front(
         hidden, norm_gain, in_weight, conv_weight, conv_bias, x_proj_weight, conv_state
     )
-    bc_raw = bc_raw.reshape(2 * N, REQ)
-    step_normed = (
-        rms_scale(step_raw.astype(F32), 1e-06, 0) * dt_norm_gain[:, None]
-    ).astype(BF16)
-    b_values = (rms_scale(bc_raw[:N], 1e-06, 0) * b_norm_gain[:, None]).T
-    c_values = (rms_scale(bc_raw[N:], 1e-06, 0) * c_norm_gain[:, None]).T
-    step_size = jax.nn.softplus(
-        jnp.dot(step_normed.T, dt_weight, preferred_element_type=F32) + dt_bias
-    )
-    decay_rates = jnp.exp(decay_log)
-    decay_factor = jnp.exp(-step_size[:, None, :] * decay_rates[None])
-    act_wide = conv_act.astype(F32)
-    new_state = (
-        decay_factor * ssm_state.astype(F32)
-        + (step_size * act_wide)[:, None, :] * b_values[:, :, None]
-    )
-    mixed_out = jnp.sum(new_state * c_values[:, :, None], axis=1) + skip_gain * act_wide
-    output = (mixed_out * jax.nn.silu(gate_half.astype(F32))).astype(BF16)
-    return (output, next_conv.transpose(1, 0, 2), new_state.astype(BF16))
+    whole = pl.BlockSpec(memory_space=pltpu.VMEM)
+    output, next_conv, next_state = pl.pallas_call(
+        state_kernel,
+        grid=(BLOCKS,),
+        out_shape=(
+            jax.ShapeDtypeStruct((REQ, LOC), BF16),
+            jax.ShapeDtypeStruct((3, REQ, LOC), BF16),
+            jax.ShapeDtypeStruct((REQ, N, LOC), BF16),
+        ),
+        in_specs=[whole] * 12 + [pl.BlockSpec((ROWS, N, LOC), lambda i: (i, 0, 0))],
+        out_specs=(
+            pl.BlockSpec((ROWS, LOC), lambda i: (i, 0)),
+            pl.BlockSpec((3, ROWS, LOC), lambda i: (0, i, 0)),
+            pl.BlockSpec((ROWS, N, LOC), lambda i: (i, 0, 0)),
+        ),
+        scratch_shapes=[
+            pltpu.VMEM((REQ, LOC), F32),
+            pltpu.VMEM((REQ, LOC), F32),
+            pltpu.VMEM((BLOCKS, N, REQ), F32),
+            pltpu.VMEM((BLOCKS, N, REQ), F32),
+        ],
+        compiler_params=pltpu.CompilerParams(vmem_limit_bytes=24 * 2**20),
+    )(
+        act,
+        mixed,
+        step_raw,
+        bc_raw.reshape(2 * N, REQ),
+        dt_norm_gain.reshape(1, DT_RANK),
+        b_norm_gain.reshape(1, N),
+        c_norm_gain.reshape(1, N),
+        dt_weight,
+        dt_bias.reshape(1, LOC),
+        decay_log,
+        skip_gain.reshape(1, LOC),
+        conv_state.transpose(1, 0, 2),
+        ssm_state,
+    )
+    return (output, next_conv.transpose(1, 0, 2), next_state)
 
 
 def solution(mesh):

time: 54.6 us -> 46.2 us (0.85)
  local copies, waits for them, and re-layouts: 6.43 us -> 0.04 us
  other arithmetic: 2.73 us -> 0 us
  Pallas kernels: 44 us -> 45.3 us
    unnamed x25 -> x18, local copies, waits for them, and re-layouts: 4.8 us -> 0.04 us
    convert_element_type x2 -> x0, other arithmetic: 2.44 us -> none  [the longest x1 1.76 us: local(): return (output, next_conv.transpose(1, 0, 2), new_state.astype(BF16))]
    pallas_call x1 -> x2, Pallas kernels: 44 us -> 45.3 us  [the longest x1 42.5 us: front(): pl.pallas_call(gather_kernel, out_shape=(pltpu.VMEM((REQ, LOC), BF16), pl...]
    exp x1 -> x0, local copies, waits for them, and re-layouts: 0.72 us -> none  [local(): decay_rates = jnp.exp(decay_log)]
    reshape x1 -> x0, local copies, waits for them, and re-layouts: 0.7 us -> none  [front(): norm_gain.reshape(1, LOC)]
where the time goes in v2:
time: 46.2 us; the launch traced here: 46.1 us
  Pallas kernels  45.3 us (98%)
  between operations  0.79 us (2%)
    pallas_call x1, Pallas kernels, front(): pl.pallas_call(gather_kernel, out_shape=(pltpu.VMEM((REQ, LOC), BF16), pl...  42.5 us
    pallas_call x1, Pallas kernels, local(): pl.pallas_call(state_kernel, grid=(BLOCKS,), out_shape=(jax.ShapeDtypeStr...  2.76 us

profile of v2, /device:TPU:8, one launch (start us, length us, event | category | flops | bytes accessed | tf_op | source)
XLA Modules:
  0.0 46.1 jit_solution(10124547830777777082)
XLA Ops:
  0.6 0.0 copy-start
  0.6 0.0 copy-start.1
  0.7 0.0 copy-start.6
  0.7 0.0 copy-start.3
  0.7 0.0 copy-start.5
  0.7 0.0 copy-start.2
  0.7 0.0 copy-start.8
  0.7 0.0 copy-start.7
  0.7 0.0 copy-start.4
  0.7 42.5 %shard_map.166 = (bf16[128,256]{1,0:T(8,128)(2,1)S(1)}, bf16[128,512]{1,0:T(8,128)(2,1)S(1)}, bf16[512,128]{1,0:T(8,128)(2,1)S(1)}, f32[32,1,128]{2,1,0:T(1,128)S(1)}) custom-call(bf16[128,256]{1,0:T(8,128)(2,1)} %hidden_hbm.1, bf16[2,128]{1,0:T(2,128)(2,1)} %bitcast.27, bf16[32768,128]{1,0:T(8,128)(2,1)} %bitcast.24, f32[4,256]{1,0:T(4,128)} %conv_weight_hbm.1, ...), custom_call_target="tpu_custom_call" | custom-call | tf_op jit(solution)/shard_map/pallas_call | solution.py:284
  43.3 0.0 copy-done
  43.3 0.0 copy-done.1
  43.3 0.0 copy-done.6
  43.3 0.0 copy-done.3
  43.3 0.0 copy-done.5
  43.3 0.0 copy-done.2
  43.3 0.0 copy-done.8
  43.3 0.0 copy-done.7
  43.4 0.0 copy-done.4
  43.4 2.8 %shard_map.167 = (bf16[128,256]{1,0:T(8,128)(2,1)}, bf16[3,128,256]{2,1,0:T(8,128)(2,1)}, bf16[128,16,256]{2,1,0:T(8,128)(2,1)}) custom-call(bf16[128,256]{1,0:T(8,128)(2,1)S(1)} %get-tuple-element.10.act, bf16[128,512]{1,0:T(8,128)(2,1)S(1)} %get-tuple-element.11.mixed, bf16[512,128]{1,0:T(8,128)(2,1)S(1)} %get-tuple-element.12.step_raw, ...), custom_call_target="tpu_custom_call" | custom-call | tf_op jit(solution)/shard_map/pallas_call | solution.py:406
Async XLA Ops:
  0.6 42.6 %copy-start = (bf16[128,16,256]{2,1,0:T(8,128)(2,1)S(1)}, bf16[128,16,256]{2,1,0:T(8,128)(2,1)}, u32[]{:S(2)}) copy-start(bf16[128,16,256]{2,1,0:T(8,128)(2,1)} %state.1) | copy-start | bytes 3145732
  0.6 42.6 %copy-start.1 = (bf16[128,3,256]{2,0,1:T(8,128)(2,1)S(1)}, bf16[128,3,256]{2,0,1:T(8,128)(2,1)}, u32[]{:S(2)}) copy-start(bf16[128,3,256]{2,0,1:T(8,128)(2,1)} %param.28) | copy-start | bytes 589828
  0.7 42.6 %copy-start.6 = (f32[256]{0:T(256)S(1)}, f32[256]{0:T(256)}, u32[]{:S(2)}) copy-start(f32[256]{0:T(256)} %param.27) | copy-start | bytes 3076
  0.7 42.6 %copy-start.3 = (f32[16,256]{1,0:T(8,128)S(1)}, f32[16,256]{1,0:T(8,128)}, u32[]{:S(2)}) copy-start(f32[16,256]{1,0:T(8,128)} %decay_log.1) | copy-start | bytes 49156
  0.7 42.6 %copy-start.5 = (f32[256]{0:T(256)S(1)}, f32[256]{0:T(256)}, u32[]{:S(2)}) copy-start(f32[256]{0:T(256)} %param.25) | copy-start | bytes 3076
  0.7 42.6 %copy-start.2 = (bf16[512,256]{1,0:T(8,128)(2,1)S(1)}, bf16[512,256]{1,0:T(8,128)(2,1)}, u32[]{:S(2)}) copy-start(bf16[512,256]{1,0:T(8,128)(2,1)} %dt_weight.1) | copy-start | bytes 786436
  0.7 42.6 %copy-start.8 = (f32[16]{0:T(128)S(1)}, f32[16]{0:T(128)}, u32[]{:S(2)}) copy-start(f32[16]{0:T(128)} %param.23) | copy-start | bytes 196
  0.7 42.6 %copy-start.7 = (f32[16]{0:T(128)S(1)}, f32[16]{0:T(128)}, u32[]{:S(2)}) copy-start(f32[16]{0:T(128)} %param.22) | copy-start | bytes 196
  0.7 42.6 %copy-start.4 = (f32[512]{0:T(512)S(1)}, f32[512]{0:T(512)}, u32[]{:S(2)}) copy-start(f32[512]{0:T(512)} %param.21) | copy-start | bytes 6148

commit v3 on v2

--- a/solution.py
+++ b/solution.py
@@ -17,37 +17,29 @@
 F32 = jnp.float32
 BF16 = jnp.bfloat16
 
-OWN = [
-    (0, 0, 1), (0, 0, -1), (0, 1, 0), (0, -1, 0), (0, 0, 2),
-    (1, 1, 0), (1, -1, 0), (1, 0, 1), (1, 0, -1), (1, 2, 0), (1, -2, 0), (1, 0, 2),
-]
-
-
-def passes():
-    along_x = [(0, 1), (0, -1), (0, 2)]
-    up, down = [(1, 0)], [(-1, 0)]
-    order = [
-        ((0, 0, -1), up + down), ((0, 0, 1), up + down), ((0, -1, 0), up), ((0, 1, 0), down),
-        ((1, -1, 0), along_x), ((1, 1, 0), along_x), ((1, 0, -1), []), ((1, 0, 1), []),
-        ((0, 0, 2), up + down),
-        ((1, -2, 0), [(1, 0), (2, 0)] + along_x), ((1, 2, 0), [(-1, 0)] + along_x), ((1, 0, 2), []),
-        ((0, -1, -1), up), ((0, 1, -1), down), ((0, -1, 1), up), ((0, 1, 1), down),
-        ((1, -1, -1), []), ((1, -1, 1), []),
-        ((0, -2, 0), [(1, 0), (2, 0)]), ((0, 2, 0), down),
-        ((1, 1, -1), []), ((1, 1, 1), []),
-        ((0, -1, 2), up), ((0, 1, 2), down),
-        ((1, -3, 0), along_x), ((1, 3, 0), along_x),
-        ((1, -1, 2), []), ((1, -2, -1), []), ((1, -2, 1), []),
-        ((0, 2, -1), down), ((0, -2, -1), [(1, 0), (2, 0)]), ((1, 2, -1), []), ((0, 2, 1), [(-1, 0), (-2, 0)]),
-        ((1, 2, 1), []),
-        ((1, 4, 0), along_x), ((0, 3, 0), []), ((1, 1, 2), []), ((0, -2, 1), up), ((1, -2, 2), []),
-        ((0, 2, 2), [(-1, 0), (-2, 0)]), ((1, 2, 2), []), ((0, -3, 0), []),
-        ((1, -3, -1), []), ((1, -3, 1), []), ((0, 3, -1), []), ((1, 3, -1), []), ((1, 3, 1), []),
-        ((0, -2, 2), up), ((0, 3, 1), []), ((0, 4, 0), []), ((1, -3, 2), []), ((1, 4, -1), []), ((1, 4, 1), []),
-        ((0, -3, -1), []), ((0, 4, 1), []), ((1, 3, 2), []), ((0, 3, 2), []), ((1, 4, 2), []),
-        ((0, -3, 1), []), ((0, 4, -1), []), ((0, 4, 2), []), ((0, -3, 2), []),
-    ]
-    return order
+GREETED = ((-2, 0), (0, 2), (2, 0), (-1, 0), (0, -1), (0, 1), (1, 0))
+OWN = (
+    (1, -1, 0), (0, 2, 0), (1, 0, -1), (1, 0, 1), (0, 0, -1), (0, 0, 1), (0, -2, 0), (0, 0, 2), (1, -2, 0),
+    (1, 0, 2), (1, 1, 0), (0, 1, 0), (1, 2, 0),
+)
+PASSES = (
+    ((1, -1, 0), ((-2, 0), (0, -1), (0, 1))), ((1, 0, -1), ((1, 0), )), ((1, 0, 1), ()),
+    ((0, 2, 0), ((0, 2), (1, 0), (0, -1), (0, 1))), ((0, 0, -1), ((1, 0), )), ((0, 0, 1), ((-1, 0), )),
+    ((1, 1, 0), ((0, 1), )), ((0, -2, 0), ((-1, 0), (0, -1), (-2, 0), (0, 2))), ((0, 1, 0), ((0, 1), )),
+    ((0, 0, 2), ()), ((1, 0, 2), ((2, 0), )), ((1, -2, 0), ((0, -1), )), ((1, 2, 0), ((1, 0), )),
+    ((1, -1, -1), ((0, -1), )), ((1, -1, 1), ((-1, 0), )), ((1, 1, -1), ((1, 0), )),
+    ((1, -3, 0), ((0, 1), (0, -1), (-1, 0))), ((0, 2, -1), ()), ((0, 2, 1), ()), ((0, 3, 0), ((0, 1), (0, -1))),
+    ((0, -1, 1), ((0, 1), (-1, 0), (0, -1))), ((0, 2, 2), ((1, 0), (-1, 0))), ((0, 1, -1), ()),
+    ((0, -3, 0), ((0, 1), )), ((0, -2, -1), ((-1, 0), (1, 0))), ((1, 1, 1), ((0, 1), (1, 0))),
+    ((1, -2, -1), ((0, -1), )), ((0, 1, 1), ()), ((1, 2, 2), ((1, 0), )), ((0, 4, 0), ((0, 1), (0, -1))),
+    ((0, -2, 2), ((-1, 0), )), ((1, 3, 0), ((0, 1), )), ((1, -2, 1), ()), ((1, -1, 2), ()),
+    ((1, -3, 1), ((0, 1), (-1, 0))), ((1, 2, -1), ((1, 0), )), ((1, 4, 0), ((0, 2), )), ((1, -3, -1), ((-1, 0), )),
+    ((0, 3, 1), ()), ((0, 3, 2), ((1, 0), )), ((0, -2, 1), ()), ((0, 3, -1), ()), ((0, -1, 2), ()),
+    ((0, -1, -1), ()), ((0, 1, 2), ()), ((0, -1, 0), ()), ((0, -3, 1), ()), ((1, 2, 1), ()), ((0, -3, -1), ()),
+    ((1, -2, 2), ()), ((1, 1, 2), ()), ((1, 3, 2), ()), ((0, -3, 2), ()), ((0, 4, -1), ()), ((0, 4, 1), ()),
+    ((1, 4, 1), ()), ((1, 3, -1), ()), ((1, 3, 1), ()), ((1, 4, -1), ()), ((0, 4, 2), ()), ((1, 4, 2), ()),
+    ((1, -3, 2), ()),
+)
 
 
 def gather_kernel(
@@ -85,10 +77,9 @@
         )
         for i in range(8)
     ]
-    greeted = [(1, 0), (-1, 0), (2, 0), (-2, 0), (0, 1), (0, -1), (0, 2)]
     barrier = pltpu.get_barrier_semaphore()
-    for dz, dx in greeted:
-        pl.semaphore_signal(barrier, inc=1, device_id=(req, place(dz, dx)), device_id_type=MESH)
+    for hz, hx in GREETED:
+        pl.semaphore_signal(barrier, inc=1, device_id=(req, place(-hz, -hx)), device_id_type=MESH)
 
     for copy in weight_copies:
         copy.start()
@@ -107,20 +98,20 @@
     )
     squares_x[pl.ds(mx, 1)] = square_row[None, :1]
 
-    pl.semaphore_wait(barrier, len(greeted))
-
-    def push(half, dz, dx, hz, hx):
-        owner = place(dz, dx)
+    pl.semaphore_wait(barrier, len(GREETED))
+
+    def push(half, z, x, hz, hx):
+        owner = place(-z, -x)
         pltpu.make_async_remote_copy(
             units.at[half, owner], units.at[half, owner], send_sem.at[half],
-            recv_sem.at[half, (dz - hz) % ZS, (dx - hx) % XS],
+            recv_sem.at[half, (z + hz) % ZS, (x + hx) % XS],
             device_id=(req, place(hz, hx)), device_id_type=MESH,
         ).start()
 
-    def await_unit(half, dz, dx):
-        owner = place(dz, dx)
+    def await_unit(half, z, x):
+        owner = place(-z, -x)
         pltpu.make_async_copy(
-            units.at[half, owner], units.at[half, owner], recv_sem.at[half, dz % ZS, dx % XS]
+            units.at[half, owner], units.at[half, owner], recv_sem.at[half, z % ZS, x % XS]
         ).wait()
 
     for half, hz, hx in OWN:
@@ -141,8 +132,8 @@
                 ].astype(BF16)
         return 0
 
-    def multiply(dz, dx, first=False):
-        owner = place(dz, dx)
+    def multiply(z, x, first=False):
+        owner = place(-z, -x)
         left = jnp.concatenate([units[0, owner], units[1, owner]], axis=1)
         product = jnp.dot(
             left, ready[pl.ds(pl.multiple_of(owner * 256, 256), 256), :], preferred_element_type=F32
@@ -164,18 +155,17 @@
     arrived = {}
     pending = []
     started = False
-    column = 0
-    order = passes()
-    for step, ((half, dz, dx), hops) in enumerate(order):
-        await_unit(half, dz, dx)
-        for hz, hx in hops:
-            push(half, dz, dx, hz, hx)
-        arrived[(dz, dx)] = arrived.get((dz, dx), 0) + 1
-        if arrived[(dz, dx)] == 2:
-            pending.append((dz, dx))
-        if dx == 0 and half == 1:
-            column += 1
-            if column == 7:
+    column = {0}
+    for (half, z, x), moves in PASSES:
+        await_unit(half, z, x)
+        for hz, hx in moves:
+            push(half, z, x, hz, hx)
+        arrived[(z, x)] = arrived.get((z, x), 0) + 1
+        if arrived[(z, x)] == 2:
+            pending.append((z, x))
+        if x == 0 and z not in column:
+            column.add(z)
+            if len(column) == ZS:
                 pltpu.make_async_copy(
                     squares_x.at[pl.ds(0, 3)], squares_x.at[pl.ds(0, 3)], sq_sem.at[1]
                 ).wait()
@@ -331,55 +321,60 @@
     )
 
 
-BLOCKS = 4
-ROWS = REQ // BLOCKS
+CHUNKS = 8
+ROWS = REQ // CHUNKS
 
 
 def state_kernel(
     act, mixed, step_raw, bc_raw, dt_gain, b_gain, c_gain, dt_weight, dt_bias, decay_log, skip_gain, conv_state, state,
-    out, next_conv, next_state,
-    step_size, drive, b_turned, c_turned,
+    out_hbm, next_conv_hbm, next_state_hbm,
+    step_size, drive, out, next_conv, next_state, sem,
 ):
-    block = pl.program_id(0)
-
-    @pl.when(block == 0)
-    def _():
-        raw = step_raw[...].astype(F32)
-        scale = lax.rsqrt(jnp.mean(raw * raw, axis=0, keepdims=True) + 1e-06)
-        normed = (jnp.transpose(raw * scale) * dt_gain[...]).astype(BF16)
-        before = jnp.dot(normed, dt_weight[...], preferred_element_type=F32) + dt_bias[...]
-        size = jnp.maximum(before, 0.0) + jnp.log1p(jnp.exp(-jnp.abs(before)))
-        step_size[...] = size
-        drive[...] = size * act[...].astype(F32)
-        square = (N, N)
-        eye = lax.broadcasted_iota(jnp.int32, square, 0) == lax.broadcasted_iota(jnp.int32, square, 1)
-        for part, gain_row, turned in ((0, b_gain, b_turned), (N, c_gain, c_turned)):
-            column = jnp.sum(
-                jnp.where(eye, jnp.broadcast_to(gain_row[...], square), 0.0), axis=1, keepdims=True
-            )
-            values = bc_raw[part : part + N]
-            scale = lax.rsqrt(jnp.mean(values * values, axis=0, keepdims=True) + 1e-06)
-            values = values * scale * column
-            for i in range(BLOCKS):
-                turned[i] = pltpu.roll(values, REQ - i * ROWS, 1) if i else values
-
-    rows = pl.ds(pl.multiple_of(block * ROWS, ROWS), ROWS)
+    next_conv[0:2] = conv_state[1:3]
+    next_conv[2] = mixed[:, :LOC]
+    conv_copy = pltpu.make_async_copy(next_conv, next_conv_hbm, sem.at[CHUNKS])
+    conv_copy.start()
+    raw = step_raw[...].astype(F32)
+    scale = lax.rsqrt(jnp.mean(raw * raw, axis=0, keepdims=True) + 1e-06)
+    normed = (jnp.transpose(raw * scale) * dt_gain[...]).astype(BF16)
+    before = jnp.dot(normed, dt_weight[...], preferred_element_type=F32) + dt_bias[...]
+    size = jnp.maximum(before, 0.0) + jnp.log1p(jnp.exp(-jnp.abs(before)))
+    step_size[...] = size
+    drive[...] = size * act[...].astype(F32)
+    square = (N, N)
+    eye = lax.broadcasted_iota(jnp.int32, square, 0) == lax.broadcasted_iota(jnp.int32, square, 1)
+    turned = []
+    for part, gain_row in ((0, b_gain), (N, c_gain)):
+        column = jnp.sum(
+            jnp.where(eye, jnp.broadcast_to(gain_row[...], square), 0.0), axis=1, keepdims=True
+        )
+        values = bc_raw[part : part + N]
+        scale = lax.rsqrt(jnp.mean(values * values, axis=0, keepdims=True) + 1e-06)
+        turned.append(values * scale * column)
+    b_turned, c_turned = turned
     rates = -jnp.exp(decay_log[...])
-    b_here = b_turned[block]
-    c_here = c_turned[block]
-    sums = []
-    for r in range(ROWS):
-        row = pl.ds(block * ROWS + r, 1)
-        decay = jnp.exp(step_size[row, :] * rates)
-        new = decay * state[r].astype(F32) + drive[row, :] * b_here[:, r : r + 1]
-        next_state[r] = new.astype(BF16)
-        sums.append(jnp.sum(new * c_here[:, r : r + 1], axis=0, keepdims=True))
-    summed = jnp.concatenate(sums, axis=0)
-    act_wide = act[rows, :].astype(F32)
-    gate = mixed[rows, LOC:].astype(F32)
-    out[...] = ((summed + skip_gain[...] * act_wide) * (gate * jax.nn.sigmoid(gate))).astype(BF16)
-    next_conv[0:2] = conv_state[1:3, rows, :]
-    next_conv[2] = mixed[rows, :LOC]
+    copies = [conv_copy]
+    for chunk in range(CHUNKS):
+        rows = slice(chunk * ROWS, chunk * ROWS + ROWS)
+        sums = []
+        for r in range(chunk * ROWS, chunk * ROWS + ROWS):
+            decay = jnp.exp(step_size[r : r + 1, :] * rates)
+            new = decay * state[r].astype(F32) + drive[r : r + 1, :] * b_turned[:, r : r + 1]
+            next_state[r] = new.astype(BF16)
+            sums.append(jnp.sum(new * c_turned[:, r : r + 1], axis=0, keepdims=True))
+        copies.append(
+            pltpu.make_async_copy(next_state.at[rows], next_state_hbm.at[rows], sem.at[chunk])
+        )
+        copies[-1].start()
+        summed = jnp.concatenate(sums, axis=0)
+        act_wide = act[rows, :].astype(F32)
+        gate = mixed[rows, LOC:].astype(F32)
+        gated = (summed + skip_gain[...] * act_wide) * (gate * jax.nn.sigmoid(gate))
+        out[rows, :] = gated.astype(BF16)
+    copies.append(pltpu.make_async_copy(out, out_hbm, sem.at[CHUNKS + 1]))
+    copies[-1].start()
+    for copy in copies:
+        copy.wait()
 
 
 def local(
@@ -405,23 +400,20 @@
     whole = pl.BlockSpec(memory_space=pltpu.VMEM)
     output, next_conv, next_state = pl.pallas_call(
         state_kernel,
-        grid=(BLOCKS,),
         out_shape=(
             jax.ShapeDtypeStruct((REQ, LOC), BF16),
             jax.ShapeDtypeStruct((3, REQ, LOC), BF16),
             jax.ShapeDtypeStruct((REQ, N, LOC), BF16),
         ),
-        in_specs=[whole] * 12 + [pl.BlockSpec((ROWS, N, LOC), lambda i: (i, 0, 0))],
-        out_specs=(
-            pl.BlockSpec((ROWS, LOC), lambda i: (i, 0)),
-            pl.BlockSpec((3, ROWS, LOC), lambda i: (0, i, 0)),
-            pl.BlockSpec((ROWS, N, LOC), lambda i: (i, 0, 0)),
-        ),
+        in_specs=[whole] * 13,
+        out_specs=(pl.BlockSpec(memory_space=pl.ANY),) * 3,
         scratch_shapes=[
             pltpu.VMEM((REQ, LOC), F32),
             pltpu.VMEM((REQ, LOC), F32),
-            pltpu.VMEM((BLOCKS, N, REQ), F32),
-            pltpu.VMEM((BLOCKS, N, REQ), F32),
+            pltpu.VMEM((REQ, LOC), BF16),
+            pltpu.VMEM((3, REQ, LOC), BF16),
+            pltpu.VMEM((REQ, N, LOC), BF16),
+            pltpu.SemaphoreType.DMA((CHUNKS + 2,)),
         ],
         compiler_params=pltpu.CompilerParams(vmem_limit_bytes=24 * 2**20),
     )(

time: 46.2 us -> 41.6 us (0.900)
  Pallas kernels: 45.3 us -> 40.7 us
    pallas_call x1, Pallas kernels: 42.5 us -> 38.6 us  [front(): pl.pallas_call(gather_kernel, out_shape=(pltpu.VMEM((REQ, LOC), BF16), pl...]
    pallas_call x1, Pallas kernels: 2.76 us -> 2.13 us  [local(): pl.pallas_call(state_kernel, out_shape=(jax.ShapeDtypeStruct((REQ, LOC),...]
where the time goes in v3:
time: 41.6 us
  Pallas kernels  40.7 us (98%)
  between operations  0.79 us (2%)
    pallas_call x1, Pallas kernels, front(): pl.pallas_call(gather_kernel, out_shape=(pltpu.VMEM((REQ, LOC), BF16), pl...  38.6 us
    pallas_call x1, Pallas kernels, local(): pl.pallas_call(state_kernel, out_shape=(jax.ShapeDtypeStruct((REQ, LOC),...  2.13 us

profile of v3, /device:TPU:8, one launch (start us, length us, event | category | flops | bytes accessed | tf_op | source)
XLA Modules:
  0.0 41.6 jit_solution(11568725230700692246)
XLA Ops:
  0.6 0.0 copy-start
  0.6 0.0 copy-start.1
  0.7 0.0 copy-start.6
  0.7 0.0 copy-start.3
  0.7 0.0 copy-start.5
  0.7 0.0 copy-start.2
  0.7 0.0 copy-start.8
  0.7 0.0 copy-start.7
  0.7 0.0 copy-start.4
  0.7 38.6 %shard_map.166 = (bf16[128,256]{1,0:T(8,128)(2,1)S(1)}, bf16[128,512]{1,0:T(8,128)(2,1)S(1)}, bf16[512,128]{1,0:T(8,128)(2,1)S(1)}, f32[32,1,128]{2,1,0:T(1,128)S(1)}) custom-call(bf16[128,256]{1,0:T(8,128)(2,1)} %hidden_hbm.1, bf16[2,128]{1,0:T(2,128)(2,1)} %bitcast.27, bf16[32768,128]{1,0:T(8,128)(2,1)} %bitcast.24, f32[4,256]{1,0:T(4,128)} %conv_weight_hbm.1, ...), custom_call_target="tpu_custom_call" | custom-call | tf_op jit(solution)/shard_map/pallas_call | solution.py:274
  39.3 0.0 copy-done
  39.3 0.0 copy-done.1
  39.4 0.0 copy-done.6
  39.4 0.0 copy-done.3
  39.4 0.0 copy-done.5
  39.4 0.0 copy-done.2
  39.4 0.0 copy-done.8
  39.4 0.0 copy-done.7
  39.4 0.0 copy-done.4
  39.4 2.1 %shard_map.167 = (bf16[128,256]{1,0:T(8,128)(2,1)}, bf16[3,128,256]{2,1,0:T(8,128)(2,1)}, bf16[128,16,256]{2,1,0:T(8,128)(2,1)}) custom-call(bf16[128,256]{1,0:T(8,128)(2,1)S(1)} %get-tuple-element.10.act, bf16[128,512]{1,0:T(8,128)(2,1)S(1)} %get-tuple-element.11.mixed, bf16[512,128]{1,0:T(8,128)(2,1)S(1)} %get-tuple-element.12.step_raw, ...), custom_call_target="tpu_custom_call" | custom-call | tf_op jit(solution)/shard_map/pallas_call | solution.py:401
Async XLA Ops:
  0.6 38.7 %copy-start = (bf16[128,16,256]{2,1,0:T(8,128)(2,1)S(1)}, bf16[128,16,256]{2,1,0:T(8,128)(2,1)}, u32[]{:S(2)}) copy-start(bf16[128,16,256]{2,1,0:T(8,128)(2,1)} %state.1) | copy-start | bytes 3145732
  0.6 38.7 %copy-start.1 = (bf16[128,3,256]{2,0,1:T(8,128)(2,1)S(1)}, bf16[128,3,256]{2,0,1:T(8,128)(2,1)}, u32[]{:S(2)}) copy-start(bf16[128,3,256]{2,0,1:T(8,128)(2,1)} %param.28) | copy-start | bytes 589828
  0.7 38.7 %copy-start.6 = (f32[256]{0:T(256)S(1)}, f32[256]{0:T(256)}, u32[]{:S(2)}) copy-start(f32[256]{0:T(256)} %param.27) | copy-start | bytes 3076
  0.7 38.7 %copy-start.3 = (f32[16,256]{1,0:T(8,128)S(1)}, f32[16,256]{1,0:T(8,128)}, u32[]{:S(2)}) copy-start(f32[16,256]{1,0:T(8,128)} %decay_log.1) | copy-start | bytes 49156
  0.7 38.7 %copy-start.5 = (f32[256]{0:T(256)S(1)}, f32[256]{0:T(256)}, u32[]{:S(2)}) copy-start(f32[256]{0:T(256)} %param.25) | copy-start | bytes 3076
  0.7 38.7 %copy-start.2 = (bf16[512,256]{1,0:T(8,128)(2,1)S(1)}, bf16[512,256]{1,0:T(8,128)(2,1)}, u32[]{:S(2)}) copy-start(bf16[512,256]{1,0:T(8,128)(2,1)} %dt_weight.1) | copy-start | bytes 786436
  0.7 38.7 %copy-start.8 = (f32[16]{0:T(128)S(1)}, f32[16]{0:T(128)}, u32[]{:S(2)}) copy-start(f32[16]{0:T(128)} %param.23) | copy-start | bytes 196
  0.7 38.7 %copy-start.7 = (f32[16]{0:T(128)S(1)}, f32[16]{0:T(128)}, u32[]{:S(2)}) copy-start(f32[16]{0:T(128)} %param.22) | copy-start | bytes 196
  0.7 38.7 %copy-start.4 = (f32[512]{0:T(512)S(1)}, f32[512]{0:T(512)}, u32[]{:S(2)}) copy-start(f32[512]{0:T(512)} %param.21) | copy-start | bytes 6148

commit v4 on v3

--- a/solution.py
+++ b/solution.py
@@ -39,6 +39,12 @@
     ((1, -2, 2), ()), ((1, 1, 2), ()), ((1, 3, 2), ()), ((0, -3, 2), ()), ((0, 4, -1), ()), ((0, 4, 1), ()),
     ((1, 4, 1), ()), ((1, 3, -1), ()), ((1, 3, 1), ()), ((1, 4, -1), ()), ((0, 4, 2), ()), ((1, 4, 2), ()),
     ((1, -3, 2), ()),
+)
+
+
+PEERS = sorted(
+    [(z, x) for z in range(-3, 5) for x in range(-1, 3) if (z, x) != (0, 0)],
+    key=lambda move: -abs(move[0]) - abs(move[1]),
 )
 
 
@@ -213,8 +219,8 @@
     def rows(index):
         return pl.ds(pl.multiple_of(index * 16, 16), 16)
 
-    def spread(i, _):
-        peer = lax.rem(me + i, DEVS)
+    for hz, hx in PEERS:
+        peer = place(hz, hx)
         pltpu.make_async_remote_copy(
             part.at[rows(peer)], got.at[rows(me)], sum_sem.at[0], sum_sem.at[1],
             device_id=(req, peer), device_id_type=MESH,
@@ -223,9 +229,6 @@
             part_bc.at[peer], got_bc.at[me], sum_sem.at[2], sum_sem.at[3],
             device_id=(req, peer), device_id_type=MESH,
         ).start()
-        return 0
-
-    lax.fori_loop(1, DEVS, spread, 0)
     got[rows(me), :] = part[rows(me), :]
     got_bc[pl.ds(me, 1)] = part_bc[pl.ds(me, 1)]
 
@@ -238,8 +241,8 @@
     step_out[rows(me), :] = step.astype(BF16)
     bc_out[pl.ds(me, 1)] = jnp.sum(got_bc[...], axis=0, keepdims=True)
 
-    def share(i, _):
-        peer = lax.rem(me + i, DEVS)
+    for hz, hx in PEERS:
+        peer = place(hz, hx)
         pltpu.make_async_remote_copy(
             step_out.at[rows(me)], step_out.at[rows(me)], out_sem.at[0], out_sem.at[1],
             device_id=(req, peer), device_id_type=MESH,
@@ -248,9 +251,6 @@
             bc_out.at[me], bc_out.at[me], out_sem.at[2], out_sem.at[3],
             device_id=(req, peer), device_id_type=MESH,
         ).start()
-        return 0
-
-    lax.fori_loop(1, DEVS, share, 0)
     for half in range(2):
         pltpu.make_async_copy(
             units.at[half, pl.ds(0, 31)], units.at[half, pl.ds(0, 31)], send_sem.at[half]

time: 41.6 us -> 40.4 us (0.971)
  Pallas kernels: 40.7 us -> 39.5 us
    pallas_call x1, Pallas kernels: 38.6 us -> 37.3 us  [front(): pl.pallas_call(gather_kernel, out_shape=(pltpu.VMEM((REQ, LOC), BF16), pl...]
where the time goes in v4:
time: 40.4 us; the launch traced here: 40.3 us
  Pallas kernels  39.5 us (98%)
  between operations  0.79 us (2%)
    pallas_call x1, Pallas kernels, front(): pl.pallas_call(gather_kernel, out_shape=(pltpu.VMEM((REQ, LOC), BF16), pl...  37.3 us
    pallas_call x1, Pallas kernels, local(): pl.pallas_call(state_kernel, out_shape=(jax.ShapeDtypeStruct((REQ, LOC),...  2.13 us

profile of v4, /device:TPU:8, one launch (start us, length us, event | category | flops | bytes accessed | tf_op | source)
XLA Modules:
  0.0 40.3 jit_solution(12817784864950142455)
XLA Ops:
  0.6 0.0 copy-start
  0.6 0.0 copy-start.1
  0.7 0.0 copy-start.6
  0.7 0.0 copy-start.3
  0.7 0.0 copy-start.5
  0.7 0.0 copy-start.2
  0.7 0.0 copy-start.8
  0.7 0.0 copy-start.7
  0.7 0.0 copy-start.4
  0.7 37.3 %shard_map.166 = (bf16[128,256]{1,0:T(8,128)(2,1)S(1)}, bf16[128,512]{1,0:T(8,128)(2,1)S(1)}, bf16[512,128]{1,0:T(8,128)(2,1)S(1)}, f32[32,1,128]{2,1,0:T(1,128)S(1)}) custom-call(bf16[128,256]{1,0:T(8,128)(2,1)} %hidden_hbm.1, bf16[2,128]{1,0:T(2,128)(2,1)} %bitcast.27, bf16[32768,128]{1,0:T(8,128)(2,1)} %bitcast.24, f32[4,256]{1,0:T(4,128)} %conv_weight_hbm.1, ...), custom_call_target="tpu_custom_call" | custom-call | tf_op jit(solution)/shard_map/pallas_call | solution.py:274
  38.1 0.0 copy-done
  38.1 0.0 copy-done.1
  38.1 0.0 copy-done.6
  38.1 0.0 copy-done.3
  38.1 0.0 copy-done.5
  38.1 0.0 copy-done.2
  38.1 0.0 copy-done.8
  38.1 0.0 copy-done.7
  38.1 0.0 copy-done.4
  38.1 2.1 %shard_map.167 = (bf16[128,256]{1,0:T(8,128)(2,1)}, bf16[3,128,256]{2,1,0:T(8,128)(2,1)}, bf16[128,16,256]{2,1,0:T(8,128)(2,1)}) custom-call(bf16[128,256]{1,0:T(8,128)(2,1)S(1)} %get-tuple-element.10.act, bf16[128,512]{1,0:T(8,128)(2,1)S(1)} %get-tuple-element.11.mixed, bf16[512,128]{1,0:T(8,128)(2,1)S(1)} %get-tuple-element.12.step_raw, ...), custom_call_target="tpu_custom_call" | custom-call | tf_op jit(solution)/shard_map/pallas_call | solution.py:401
Async XLA Ops:
  0.6 37.4 %copy-start = (bf16[128,16,256]{2,1,0:T(8,128)(2,1)S(1)}, bf16[128,16,256]{2,1,0:T(8,128)(2,1)}, u32[]{:S(2)}) copy-start(bf16[128,16,256]{2,1,0:T(8,128)(2,1)} %state.1) | copy-start | bytes 3145732
  0.6 37.4 %copy-start.1 = (bf16[128,3,256]{2,0,1:T(8,128)(2,1)S(1)}, bf16[128,3,256]{2,0,1:T(8,128)(2,1)}, u32[]{:S(2)}) copy-start(bf16[128,3,256]{2,0,1:T(8,128)(2,1)} %param.28) | copy-start | bytes 589828
  0.7 37.4 %copy-start.6 = (f32[256]{0:T(256)S(1)}, f32[256]{0:T(256)}, u32[]{:S(2)}) copy-start(f32[256]{0:T(256)} %param.27) | copy-start | bytes 3076
  0.7 37.4 %copy-start.3 = (f32[16,256]{1,0:T(8,128)S(1)}, f32[16,256]{1,0:T(8,128)}, u32[]{:S(2)}) copy-start(f32[16,256]{1,0:T(8,128)} %decay_log.1) | copy-start | bytes 49156
  0.7 37.4 %copy-start.5 = (f32[256]{0:T(256)S(1)}, f32[256]{0:T(256)}, u32[]{:S(2)}) copy-start(f32[256]{0:T(256)} %param.25) | copy-start | bytes 3076
  0.7 37.4 %copy-start.2 = (bf16[512,256]{1,0:T(8,128)(2,1)S(1)}, bf16[512,256]{1,0:T(8,128)(2,1)}, u32[]{:S(2)}) copy-start(bf16[512,256]{1,0:T(8,128)(2,1)} %dt_weight.1) | copy-start | bytes 786436
  0.7 37.4 %copy-start.8 = (f32[16]{0:T(128)S(1)}, f32[16]{0:T(128)}, u32[]{:S(2)}) copy-start(f32[16]{0:T(128)} %param.23) | copy-start | bytes 196
  0.7 37.4 %copy-start.7 = (f32[16]{0:T(128)S(1)}, f32[16]{0:T(128)}, u32[]{:S(2)}) copy-start(f32[16]{0:T(128)} %param.22) | copy-start | bytes 196
  0.7 37.4 %copy-start.4 = (f32[512]{0:T(512)S(1)}, f32[512]{0:T(512)}, u32[]{:S(2)}) copy-start(f32[512]{0:T(512)} %param.21) | copy-start | bytes 6148

commit v5 on v4

--- a/solution.py
+++ b/solution.py
@@ -51,7 +51,7 @@
 def gather_kernel(
     hidden_hbm, gain_hbm, weight_hbm, conv_weight_hbm, conv_bias_hbm, proj_hbm, conv_state_hbm,
     act_out, mixed_out, step_out, bc_out,
-    hidden, gain, conv_weight, conv_bias, proj, conv_state, raw, wide, ready, units, total, squares_x, squares_z, part, part_bc, got, got_bc,
+    hidden, gain, conv_weight, conv_bias, proj, conv_state, raw, wide, ready, units, total, squares_x, squares_z, inverse, window, part, part_bc, got, got_bc,
     in_sem, weight_sem, recv_sem, send_sem, sq_sem, sum_sem, out_sem,
 ):
     req = lax.axis_index("req")
@@ -157,12 +157,24 @@
             lax.fori_loop(converted, last, convert, 0)
             converted = last
 
+    def settle():
+        for copy in small_copies[2:]:
+            copy.wait()
+        pltpu.make_async_copy(
+            squares_z.at[pl.ds(0, 7)], squares_z.at[pl.ds(0, 7)], sq_sem.at[3]
+        ).wait()
+        inverse_row = lax.rsqrt(jnp.sum(squares_z[...], axis=0) / D + 1e-05)
+        inverse[...] = jnp.transpose(jnp.broadcast_to(inverse_row, (128, 128)))
+        older = conv_state[0].astype(F32) * conv_weight[0:1]
+        older += conv_state[1].astype(F32) * conv_weight[1:2]
+        window[...] = older + conv_state[2].astype(F32) * conv_weight[2:3]
+
     convert_to(8)
     arrived = {}
     pending = []
     started = False
     column = {0}
-    for (half, z, x), moves in PASSES:
+    for step, ((half, z, x), moves) in enumerate(PASSES):
         await_unit(half, z, x)
         for hz, hx in moves:
             push(half, z, x, hz, hx)
@@ -188,26 +200,18 @@
                 multiply(0, 0, True)
                 started = True
             multiply(*pending.pop(0))
+        if step == len(PASSES) - 5:
+            settle()
     while pending:
         multiply(*pending.pop(0))
 
-    pltpu.make_async_copy(squares_z.at[pl.ds(0, 7)], squares_z.at[pl.ds(0, 7)], sq_sem.at[3]).wait()
-    row = jnp.sum(squares_z[...], axis=0)
-    inverse_row = lax.rsqrt(row / D + 1e-05)
-    inverse = jnp.transpose(jnp.broadcast_to(inverse_row, (128, 128)))
-    for copy in small_copies[2:]:
-        copy.wait()
     mixed = [
-        (total[:, i * 128 : i * 128 + 128] * inverse).astype(BF16) for i in range(4)
+        (total[:, i * 128 : i * 128 + 128] * inverse[...]).astype(BF16) for i in range(4)
     ]
     new_inputs = jnp.concatenate(mixed[:2], axis=1)
     mixed_out[...] = jnp.concatenate(mixed, axis=1)
-    window = conv_state[0].astype(F32) * conv_weight[0:1]
-    window += conv_state[1].astype(F32) * conv_weight[1:2]
-    window += conv_state[2].astype(F32) * conv_weight[2:3]
-    window += new_inputs.astype(F32) * conv_weight[3:4]
-    window += conv_bias[...]
-    act = (window * jax.nn.sigmoid(window)).astype(BF16)
+    summed = window[...] + new_inputs.astype(F32) * conv_weight[3:4] + conv_bias[...]
+    act = (summed * jax.nn.sigmoid(summed)).astype(BF16)
     act_out[...] = act
     projected = lax.dot_general(
         proj[...], act, (((1,), (1,)), ((), ())), preferred_element_type=F32
@@ -235,10 +239,10 @@
     some, some_bc = pl.ds(0, 31 * 16), pl.ds(0, 31)
     pltpu.make_async_copy(got.at[some], got.at[some], sum_sem.at[1]).wait()
     pltpu.make_async_copy(got_bc.at[some_bc], got_bc.at[some_bc], sum_sem.at[3]).wait()
-    step = got[0:16].astype(F32)
+    reduced = got[0:16].astype(F32)
     for i in range(1, DEVS):
-        step += got[i * 16 : i * 16 + 16].astype(F32)
-    step_out[rows(me), :] = step.astype(BF16)
+        reduced += got[i * 16 : i * 16 + 16].astype(F32)
+    step_out[rows(me), :] = reduced.astype(BF16)
     bc_out[pl.ds(me, 1)] = jnp.sum(got_bc[...], axis=0, keepdims=True)
 
     for hz, hx in PEERS:
@@ -295,6 +299,8 @@
             pltpu.VMEM((REQ, 2 * LOC), F32),
             pltpu.VMEM((XS, 1, REQ), F32),
             pltpu.VMEM((ZS, 1, REQ), F32),
+            pltpu.VMEM((128, 128), F32),
+            pltpu.VMEM((REQ, LOC), F32),
             pltpu.VMEM((DT_RANK, REQ), BF16),
             pltpu.VMEM((2 * N, 1, REQ), F32),
             pltpu.VMEM((DT_RANK, REQ), BF16),

time: 40.4 us -> 40.1 us (level)
  no operation moved by 1% of the time
where the time goes in v5:
time: 40.1 us; the launch traced here: 40 us
  Pallas kernels  39.2 us (98%)
  between operations  0.79 us (2%)
    pallas_call x1, Pallas kernels, front(): pl.pallas_call(gather_kernel, out_shape=(pltpu.VMEM((REQ, LOC), BF16), pl...  37 us
    pallas_call x1, Pallas kernels, local(): pl.pallas_call(state_kernel, out_shape=(jax.ShapeDtypeStruct((REQ, LOC),...  2.13 us

profile of v5, /device:TPU:8, one launch (start us, length us, event | category | flops | bytes accessed | tf_op | source)
XLA Modules:
  0.0 40.0 jit_solution(8860278765548454617)
XLA Ops:
  0.6 0.0 copy-start
  0.6 0.0 copy-start.1
  0.7 0.0 copy-start.6
  0.7 0.0 copy-start.3
  0.7 0.0 copy-start.5
  0.7 0.0 copy-start.2
  0.7 0.0 copy-start.8
  0.7 0.0 copy-start.7
  0.7 0.0 copy-start.4
  0.7 37.0 %shard_map.166 = (bf16[128,256]{1,0:T(8,128)(2,1)S(1)}, bf16[128,512]{1,0:T(8,128)(2,1)S(1)}, bf16[512,128]{1,0:T(8,128)(2,1)S(1)}, f32[32,1,128]{2,1,0:T(1,128)S(1)}) custom-call(bf16[128,256]{1,0:T(8,128)(2,1)} %hidden_hbm.1, bf16[2,128]{1,0:T(2,128)(2,1)} %bitcast.27, bf16[32768,128]{1,0:T(8,128)(2,1)} %bitcast.24, f32[4,256]{1,0:T(4,128)} %conv_weight_hbm.1, ...), custom_call_target="tpu_custom_call" | custom-call | tf_op jit(solution)/shard_map/pallas_call | solution.py:278
  37.8 0.0 copy-done
  37.8 0.0 copy-done.1
  37.8 0.0 copy-done.6
  37.8 0.0 copy-done.3
  37.8 0.0 copy-done.5
  37.8 0.0 copy-done.2
  37.8 0.0 copy-done.8
  37.8 0.0 copy-done.7
  37.8 0.0 copy-done.4
  37.9 2.1 %shard_map.167 = (bf16[128,256]{1,0:T(8,128)(2,1)}, bf16[3,128,256]{2,1,0:T(8,128)(2,1)}, bf16[128,16,256]{2,1,0:T(8,128)(2,1)}) custom-call(bf16[128,256]{1,0:T(8,128)(2,1)S(1)} %get-tuple-element.10.act, bf16[128,512]{1,0:T(8,128)(2,1)S(1)} %get-tuple-element.11.mixed, bf16[512,128]{1,0:T(8,128)(2,1)S(1)} %get-tuple-element.12.step_raw, ...), custom_call_target="tpu_custom_call" | custom-call | tf_op jit(solution)/shard_map/pallas_call | solution.py:407
Async XLA Ops:
  0.6 37.1 %copy-start = (bf16[128,16,256]{2,1,0:T(8,128)(2,1)S(1)}, bf16[128,16,256]{2,1,0:T(8,128)(2,1)}, u32[]{:S(2)}) copy-start(bf16[128,16,256]{2,1,0:T(8,128)(2,1)} %state.1) | copy-start | bytes 3145732
  0.6 37.1 %copy-start.1 = (bf16[128,3,256]{2,0,1:T(8,128)(2,1)S(1)}, bf16[128,3,256]{2,0,1:T(8,128)(2,1)}, u32[]{:S(2)}) copy-start(bf16[128,3,256]{2,0,1:T(8,128)(2,1)} %param.28) | copy-start | bytes 589828
  0.7 37.1 %copy-start.6 = (f32[256]{0:T(256)S(1)}, f32[256]{0:T(256)}, u32[]{:S(2)}) copy-start(f32[256]{0:T(256)} %param.27) | copy-start | bytes 3076
  0.7 37.1 %copy-start.3 = (f32[16,256]{1,0:T(8,128)S(1)}, f32[16,256]{1,0:T(8,128)}, u32[]{:S(2)}) copy-start(f32[16,256]{1,0:T(8,128)} %decay_log.1) | copy-start | bytes 49156
  0.7 37.1 %copy-start.5 = (f32[256]{0:T(256)S(1)}, f32[256]{0:T(256)}, u32[]{:S(2)}) copy-start(f32[256]{0:T(256)} %param.25) | copy-start | bytes 3076
  0.7 37.1 %copy-start.2 = (bf16[512,256]{1,0:T(8,128)(2,1)S(1)}, bf16[512,256]{1,0:T(8,128)(2,1)}, u32[]{:S(2)}) copy-start(bf16[512,256]{1,0:T(8,128)(2,1)} %dt_weight.1) | copy-start | bytes 786436
  0.7 37.1 %copy-start.8 = (f32[16]{0:T(128)S(1)}, f32[16]{0:T(128)}, u32[]{:S(2)}) copy-start(f32[16]{0:T(128)} %param.23) | copy-start | bytes 196
  0.7 37.1 %copy-start.7 = (f32[16]{0:T(128)S(1)}, f32[16]{0:T(128)}, u32[]{:S(2)}) copy-start(f32[16]{0:T(128)} %param.22) | copy-start | bytes 196
  0.7 37.1 %copy-start.4 = (f32[512]{0:T(512)S(1)}, f32[512]{0:T(512)}, u32[]{:S(2)}) copy-start(f32[512]{0:T(512)} %param.21) | copy-start | bytes 6148

commit v6 on v5

--- a/solution.py
+++ b/solution.py
@@ -334,7 +334,7 @@
 def state_kernel(
     act, mixed, step_raw, bc_raw, dt_gain, b_gain, c_gain, dt_weight, dt_bias, decay_log, skip_gain, conv_state, state,
     out_hbm, next_conv_hbm, next_state_hbm,
-    step_size, drive, out, next_conv, next_state, sem,
+    step_size, drive, folded, out, next_conv, next_state, sem,
 ):
     next_conv[0:2] = conv_state[1:3]
     next_conv[2] = mixed[:, :LOC]
@@ -362,17 +362,26 @@
     copies = [conv_copy]
     for chunk in range(CHUNKS):
         rows = slice(chunk * ROWS, chunk * ROWS + ROWS)
-        sums = []
         for r in range(chunk * ROWS, chunk * ROWS + ROWS):
             decay = jnp.exp(step_size[r : r + 1, :] * rates)
             new = decay * state[r].astype(F32) + drive[r : r + 1, :] * b_turned[:, r : r + 1]
             next_state[r] = new.astype(BF16)
-            sums.append(jnp.sum(new * c_turned[:, r : r + 1], axis=0, keepdims=True))
+            weighted = new * c_turned[:, r : r + 1]
+            for tile in range(2):
+                lanes = slice(tile * 128, tile * 128 + 128)
+                folded[tile, r * 8 : r * 8 + 8] = weighted[:8, lanes] + weighted[8:, lanes]
         copies.append(
             pltpu.make_async_copy(next_state.at[rows], next_state_hbm.at[rows], sem.at[chunk])
         )
         copies[-1].start()
-        summed = jnp.concatenate(sums, axis=0)
+        first = chunk * ROWS * 8
+        halves = []
+        for tile in range(2):
+            half = folded[tile, pl.ds(first, ROWS, stride=8), :]
+            for i in range(1, 8):
+                half += folded[tile, pl.ds(first + i, ROWS, stride=8), :]
+            halves.append(half)
+        summed = jnp.concatenate(halves, axis=1)
         act_wide = act[rows, :].astype(F32)
         gate = mixed[rows, LOC:].astype(F32)
         gated = (summed + skip_gain[...] * act_wide) * (gate * jax.nn.sigmoid(gate))
@@ -416,6 +425,7 @@
         scratch_shapes=[
             pltpu.VMEM((REQ, LOC), F32),
             pltpu.VMEM((REQ, LOC), F32),
+            pltpu.VMEM((2, REQ * 8, 128), F32),
             pltpu.VMEM((REQ, LOC), BF16),
             pltpu.VMEM((3, REQ, LOC), BF16),
             pltpu.VMEM((REQ, N, LOC), BF16),

time: 40.1 us -> 40 us (level)
  no operation moved by 1% of the time
where the time goes in v6:
time: 40 us; the launch traced here: 39.9 us
  Pallas kernels  39 us (98%)
  between operations  0.79 us (2%)
    pallas_call x1, Pallas kernels, front(): pl.pallas_call(gather_kernel, out_shape=(pltpu.VMEM((REQ, LOC), BF16), pl...  37 us
    pallas_call x1, Pallas kernels, local(): pl.pallas_call(state_kernel, out_shape=(jax.ShapeDtypeStruct((REQ, LOC),...  2.02 us

profile of v6, /device:TPU:8, one launch (start us, length us, event | category | flops | bytes accessed | tf_op | source)
XLA Modules:
  0.0 39.9 jit_solution(4761018234103231505)
XLA Ops:
  0.6 0.0 copy-start
  0.6 0.0 copy-start.1
  0.7 0.0 copy-start.6
  0.7 0.0 copy-start.3
  0.7 0.0 copy-start.5
  0.7 0.0 copy-start.2
  0.7 0.0 copy-start.8
  0.7 0.0 copy-start.7
  0.7 0.0 copy-start.4
  0.7 37.0 %shard_map.166 = (bf16[128,256]{1,0:T(8,128)(2,1)S(1)}, bf16[128,512]{1,0:T(8,128)(2,1)S(1)}, bf16[512,128]{1,0:T(8,128)(2,1)S(1)}, f32[32,1,128]{2,1,0:T(1,128)S(1)}) custom-call(bf16[128,256]{1,0:T(8,128)(2,1)} %hidden_hbm.1, bf16[2,128]{1,0:T(2,128)(2,1)} %bitcast.27, bf16[32768,128]{1,0:T(8,128)(2,1)} %bitcast.24, f32[4,256]{1,0:T(4,128)} %conv_weight_hbm.1, ...), custom_call_target="tpu_custom_call" | custom-call | tf_op jit(solution)/shard_map/pallas_call | solution.py:278
  37.8 0.0 copy-done
  37.8 0.0 copy-done.1
  37.8 0.0 copy-done.6
  37.8 0.0 copy-done.3
  37.8 0.0 copy-done.5
  37.8 0.0 copy-done.2
  37.8 0.0 copy-done.8
  37.8 0.0 copy-done.7
  37.8 0.0 copy-done.4
  37.9 2.0 %shard_map.167 = (bf16[128,256]{1,0:T(8,128)(2,1)}, bf16[3,128,256]{2,1,0:T(8,128)(2,1)}, bf16[128,16,256]{2,1,0:T(8,128)(2,1)}) custom-call(bf16[128,256]{1,0:T(8,128)(2,1)S(1)} %get-tuple-element.10.act, bf16[128,512]{1,0:T(8,128)(2,1)S(1)} %get-tuple-element.11.mixed, bf16[512,128]{1,0:T(8,128)(2,1)S(1)} %get-tuple-element.12.step_raw, ...), custom_call_target="tpu_custom_call" | custom-call | tf_op jit(solution)/shard_map/pallas_call | solution.py:416
Async XLA Ops:
  0.6 37.1 %copy-start = (bf16[128,16,256]{2,1,0:T(8,128)(2,1)S(1)}, bf16[128,16,256]{2,1,0:T(8,128)(2,1)}, u32[]{:S(2)}) copy-start(bf16[128,16,256]{2,1,0:T(8,128)(2,1)} %state.1) | copy-start | bytes 3145732
  0.6 37.1 %copy-start.1 = (bf16[128,3,256]{2,0,1:T(8,128)(2,1)S(1)}, bf16[128,3,256]{2,0,1:T(8,128)(2,1)}, u32[]{:S(2)}) copy-start(bf16[128,3,256]{2,0,1:T(8,128)(2,1)} %param.28) | copy-start | bytes 589828
  0.7 37.1 %copy-start.6 = (f32[256]{0:T(256)S(1)}, f32[256]{0:T(256)}, u32[]{:S(2)}) copy-start(f32[256]{0:T(256)} %param.27) | copy-start | bytes 3076
  0.7 37.1 %copy-start.3 = (f32[16,256]{1,0:T(8,128)S(1)}, f32[16,256]{1,0:T(8,128)}, u32[]{:S(2)}) copy-start(f32[16,256]{1,0:T(8,128)} %decay_log.1) | copy-start | bytes 49156
  0.7 37.1 %copy-start.5 = (f32[256]{0:T(256)S(1)}, f32[256]{0:T(256)}, u32[]{:S(2)}) copy-start(f32[256]{0:T(256)} %param.25) | copy-start | bytes 3076
  0.7 37.1 %copy-start.2 = (bf16[512,256]{1,0:T(8,128)(2,1)S(1)}, bf16[512,256]{1,0:T(8,128)(2,1)}, u32[]{:S(2)}) copy-start(bf16[512,256]{1,0:T(8,128)(2,1)} %dt_weight.1) | copy-start | bytes 786436
  0.7 37.1 %copy-start.8 = (f32[16]{0:T(128)S(1)}, f32[16]{0:T(128)}, u32[]{:S(2)}) copy-start(f32[16]{0:T(128)} %param.23) | copy-start | bytes 196
  0.7 37.1 %copy-start.7 = (f32[16]{0:T(128)S(1)}, f32[16]{0:T(128)}, u32[]{:S(2)}) copy-start(f32[16]{0:T(128)} %param.22) | copy-start | bytes 196
  0.7 37.1 %copy-start.4 = (f32[512]{0:T(512)S(1)}, f32[512]{0:T(512)}, u32[]{:S(2)}) copy-start(f32[512]{0:T(512)} %param.21) | copy-start | bytes 6148

commit v7 on v6

--- a/solution.py
+++ b/solution.py
@@ -23,22 +23,21 @@
     (1, 0, 2), (1, 1, 0), (0, 1, 0), (1, 2, 0),
 )
 PASSES = (
-    ((1, -1, 0), ((-2, 0), (0, -1), (0, 1))), ((1, 0, -1), ((1, 0), )), ((1, 0, 1), ()),
+    ((1, -1, 0), ((-2, 0), (0, -1), (0, 1))), ((1, 0, -1), ((1, 0), )),
     ((0, 2, 0), ((0, 2), (1, 0), (0, -1), (0, 1))), ((0, 0, -1), ((1, 0), )), ((0, 0, 1), ((-1, 0), )),
     ((1, 1, 0), ((0, 1), )), ((0, -2, 0), ((-1, 0), (0, -1), (-2, 0), (0, 2))), ((0, 1, 0), ((0, 1), )),
-    ((0, 0, 2), ()), ((1, 0, 2), ((2, 0), )), ((1, -2, 0), ((0, -1), )), ((1, 2, 0), ((1, 0), )),
+    ((1, 0, 2), ((2, 0), )), ((1, 0, 1), ()), ((1, -2, 0), ((0, -1), )), ((1, 2, 0), ((1, 0), )),
     ((1, -1, -1), ((0, -1), )), ((1, -1, 1), ((-1, 0), )), ((1, 1, -1), ((1, 0), )),
-    ((1, -3, 0), ((0, 1), (0, -1), (-1, 0))), ((0, 2, -1), ()), ((0, 2, 1), ()), ((0, 3, 0), ((0, 1), (0, -1))),
-    ((0, -1, 1), ((0, 1), (-1, 0), (0, -1))), ((0, 2, 2), ((1, 0), (-1, 0))), ((0, 1, -1), ()),
-    ((0, -3, 0), ((0, 1), )), ((0, -2, -1), ((-1, 0), (1, 0))), ((1, 1, 1), ((0, 1), (1, 0))),
-    ((1, -2, -1), ((0, -1), )), ((0, 1, 1), ()), ((1, 2, 2), ((1, 0), )), ((0, 4, 0), ((0, 1), (0, -1))),
-    ((0, -2, 2), ((-1, 0), )), ((1, 3, 0), ((0, 1), )), ((1, -2, 1), ()), ((1, -1, 2), ()),
-    ((1, -3, 1), ((0, 1), (-1, 0))), ((1, 2, -1), ((1, 0), )), ((1, 4, 0), ((0, 2), )), ((1, -3, -1), ((-1, 0), )),
-    ((0, 3, 1), ()), ((0, 3, 2), ((1, 0), )), ((0, -2, 1), ()), ((0, 3, -1), ()), ((0, -1, 2), ()),
-    ((0, -1, -1), ()), ((0, 1, 2), ()), ((0, -1, 0), ()), ((0, -3, 1), ()), ((1, 2, 1), ()), ((0, -3, -1), ()),
-    ((1, -2, 2), ()), ((1, 1, 2), ()), ((1, 3, 2), ()), ((0, -3, 2), ()), ((0, 4, -1), ()), ((0, 4, 1), ()),
-    ((1, 4, 1), ()), ((1, 3, -1), ()), ((1, 3, 1), ()), ((1, 4, -1), ()), ((0, 4, 2), ()), ((1, 4, 2), ()),
-    ((1, -3, 2), ()),
+    ((1, -3, 0), ((0, 1), (0, -1), (-1, 0))), ((0, 0, 2), ()), ((0, 3, 0), ((0, 1), (0, -1))),
+    ((0, -1, 1), ((0, 1), (-1, 0), (0, -1))), ((0, 2, 2), ((1, 0), (-1, 0))), ((0, -3, 0), ((0, 1), )),
+    ((0, -2, -1), ((-1, 0), (1, 0))), ((1, 1, 1), ((0, 1), (1, 0))), ((0, 2, -1), ()), ((1, -2, -1), ((0, -1), )),
+    ((0, 2, 1), ()), ((1, 2, 2), ((1, 0), )), ((0, 4, 0), ((0, 1), (0, -1))), ((0, -2, 2), ((-1, 0), )),
+    ((0, 1, -1), ()), ((1, 3, 0), ((0, 1), )), ((1, -3, 1), ((0, 1), (-1, 0))), ((1, 2, -1), ((1, 0), )),
+    ((0, 1, 1), ()), ((1, 4, 0), ((0, 2), )), ((1, -3, -1), ((-1, 0), )), ((0, 3, 2), ((1, 0), )), ((1, -2, 1), ()),
+    ((1, -1, 2), ()), ((0, 3, 1), ()), ((0, -2, 1), ()), ((0, 3, -1), ()), ((0, -1, 2), ()), ((0, -1, -1), ()),
+    ((0, 1, 2), ()), ((0, -1, 0), ()), ((0, -3, 1), ()), ((1, 2, 1), ()), ((0, -3, -1), ()), ((1, -2, 2), ()),
+    ((1, 1, 2), ()), ((1, 3, 2), ()), ((0, -3, 2), ()), ((0, 4, -1), ()), ((0, 4, 1), ()), ((1, 4, 1), ()),
+    ((1, 3, -1), ()), ((1, 3, 1), ()), ((1, 4, -1), ()), ((0, 4, 2), ()), ((1, 4, 2), ()), ((1, -3, 2), ()),
 )
 
 

time: 40 us -> 39.9 us (level)
  no operation moved by 1% of the time
where the time goes in v7:
time: 39.9 us; the launch traced here: 39.8 us
  Pallas kernels  39 us (98%)
  between operations  0.79 us (2%)
    pallas_call x1, Pallas kernels, front(): pl.pallas_call(gather_kernel, out_shape=(pltpu.VMEM((REQ, LOC), BF16), pl...  37 us
    pallas_call x1, Pallas kernels, local(): pl.pallas_call(state_kernel, out_shape=(jax.ShapeDtypeStruct((REQ, LOC),...  2.02 us

profile of v7, /device:TPU:8, one launch (start us, length us, event | category | flops | bytes accessed | tf_op | source)
XLA Modules:
  0.0 39.8 jit_solution(4568528429454472982)
XLA Ops:
  0.6 0.0 copy-start
  0.6 0.0 copy-start.1
  0.7 0.0 copy-start.6
  0.7 0.0 copy-start.3
  0.7 0.0 copy-start.5
  0.7 0.0 copy-start.2
  0.7 0.0 copy-start.8
  0.7 0.0 copy-start.7
  0.7 0.0 copy-start.4
  0.7 37.0 %shard_map.166 = (bf16[128,256]{1,0:T(8,128)(2,1)S(1)}, bf16[128,512]{1,0:T(8,128)(2,1)S(1)}, bf16[512,128]{1,0:T(8,128)(2,1)S(1)}, f32[32,1,128]{2,1,0:T(1,128)S(1)}) custom-call(bf16[128,256]{1,0:T(8,128)(2,1)} %hidden_hbm.1, bf16[2,128]{1,0:T(2,128)(2,1)} %bitcast.27, bf16[32768,128]{1,0:T(8,128)(2,1)} %bitcast.24, f32[4,256]{1,0:T(4,128)} %conv_weight_hbm.1, ...), custom_call_target="tpu_custom_call" | custom-call | tf_op jit(solution)/shard_map/pallas_call | solution.py:277
  37.7 0.0 copy-done
  37.7 0.0 copy-done.1
  37.7 0.0 copy-done.6
  37.7 0.0 copy-done.3
  37.7 0.0 copy-done.5
  37.7 0.0 copy-done.2
  37.7 0.0 copy-done.8
  37.8 0.0 copy-done.7
  37.8 0.0 copy-done.4
  37.8 2.0 %shard_map.167 = (bf16[128,256]{1,0:T(8,128)(2,1)}, bf16[3,128,256]{2,1,0:T(8,128)(2,1)}, bf16[128,16,256]{2,1,0:T(8,128)(2,1)}) custom-call(bf16[128,256]{1,0:T(8,128)(2,1)S(1)} %get-tuple-element.10.act, bf16[128,512]{1,0:T(8,128)(2,1)S(1)} %get-tuple-element.11.mixed, bf16[512,128]{1,0:T(8,128)(2,1)S(1)} %get-tuple-element.12.step_raw, ...), custom_call_target="tpu_custom_call" | custom-call | tf_op jit(solution)/shard_map/pallas_call | solution.py:415
Async XLA Ops:
  0.6 37.1 %copy-start = (bf16[128,16,256]{2,1,0:T(8,128)(2,1)S(1)}, bf16[128,16,256]{2,1,0:T(8,128)(2,1)}, u32[]{:S(2)}) copy-start(bf16[128,16,256]{2,1,0:T(8,128)(2,1)} %state.1) | copy-start | bytes 3145732
  0.6 37.1 %copy-start.1 = (bf16[128,3,256]{2,0,1:T(8,128)(2,1)S(1)}, bf16[128,3,256]{2,0,1:T(8,128)(2,1)}, u32[]{:S(2)}) copy-start(bf16[128,3,256]{2,0,1:T(8,128)(2,1)} %param.28) | copy-start | bytes 589828
  0.7 37.1 %copy-start.6 = (f32[256]{0:T(256)S(1)}, f32[256]{0:T(256)}, u32[]{:S(2)}) copy-start(f32[256]{0:T(256)} %param.27) | copy-start | bytes 3076
  0.7 37.1 %copy-start.3 = (f32[16,256]{1,0:T(8,128)S(1)}, f32[16,256]{1,0:T(8,128)}, u32[]{:S(2)}) copy-start(f32[16,256]{1,0:T(8,128)} %decay_log.1) | copy-start | bytes 49156
  0.7 37.1 %copy-start.5 = (f32[256]{0:T(256)S(1)}, f32[256]{0:T(256)}, u32[]{:S(2)}) copy-start(f32[256]{0:T(256)} %param.25) | copy-start | bytes 3076
  0.7 37.1 %copy-start.2 = (bf16[512,256]{1,0:T(8,128)(2,1)S(1)}, bf16[512,256]{1,0:T(8,128)(2,1)}, u32[]{:S(2)}) copy-start(bf16[512,256]{1,0:T(8,128)(2,1)} %dt_weight.1) | copy-start | bytes 786436
  0.7 37.1 %copy-start.8 = (f32[16]{0:T(128)S(1)}, f32[16]{0:T(128)}, u32[]{:S(2)}) copy-start(f32[16]{0:T(128)} %param.23) | copy-start | bytes 196
  0.7 37.1 %copy-start.7 = (f32[16]{0:T(128)S(1)}, f32[16]{0:T(128)}, u32[]{:S(2)}) copy-start(f32[16]{0:T(128)} %param.22) | copy-start | bytes 196
  0.7 37.1 %copy-start.4 = (f32[512]{0:T(512)S(1)}, f32[512]{0:T(512)}, u32[]{:S(2)}) copy-start(f32[512]{0:T(512)} %param.21) | copy-start | bytes 6148
